TPU v7x, 32 devices: a whole 2x2x4 slice. The times are simulated.
32 devices in a mesh: groups: 2 (over y), row: 8 (over z, x), col: 2 (over core).
Axes of the slice: x: 2, y: 2, z: 4, core: 2. Of those that a mesh axis runs over, the one named last changes fastest.
Arguments:
- sketch: int32 [64, 65536], P(None, ('groups', 'row', 'col')), parts along dimension 1, may hold values from -1 to 1, as said below
- tile_row: int32 [16, 2, 64], P(('groups', 'row'), 'col'), parts along dimension 0, may hold values from 0 to 127, as said below
- tile_col: int32 [16, 2, 64], P(('groups', 'row'), 'col'), parts along dimension 0, may hold values from 0 to 127, as said below
- tile_count: int32 [16, 2], P(('groups', 'row'), 'col'), parts along dimension 0, may hold values from 32 to 64, as said below
- neighbors: int32 [16, 2, 64, 16, 256], P(('groups', 'row'), 'col'), parts along dimension 0, may hold values from 0 to 255
- weights: bfloat16 [16, 2, 64, 16, 256], P(('groups', 'row'), 'col'), parts along dimension 0, may hold values from 0.005 to 1.125
Outputs:
- solution: float32 [64, 65536], P(None, ('groups', 'row', 'col')), parts along dimension 1
- residual: float32 [64, 65536], P(None, ('groups', 'row', 'col')), parts along dimension 1
There are 2 independent parts, one for each index of `groups`. A program takes and returns all parts, laid end to end along the dimension named above; each array names one. Nothing has to cross between parts.
Inputs may be any that keep to these rules, and one draw needn't show every extreme that they name: `sketch`: each entry is -1 or 1. `tile_row`: device (r, c) of the row and col axes holds tiles whose block row is one of its own 8 row blocks, (2 r + c) * 8 to (2 r + c + 1) * 8 - 1. Each of these row blocks has its diagonal tile in a live slot and 4 to 8 live tiles; live slots come first. `tile_col`: A tile's block column is min(tile_row + d, 127) with 0 <= d < 16. `tile_count`: some device has all 64 slots live.
All inputs are finite; a program needn't handle non-finite values.
Results may differ from a plain program's by a relative error of at most 0.0003.
Values sent between devices are 32-bit elements; how exact they have to be, the bound alone decides.
A program may use at most 128 MiB of HBM per device.

v0:
```python
import functools
import jax
import jax.numpy as jnp
from jax import lax
from jax.experimental import pallas as pl
from jax.experimental.pallas import tpu as pltpu
from jax.sharding import PartitionSpec as P

ridge_term = 1.0
build_group = 4
apply_group = 8
reach = 15
nt = (((1,), (1,)), ((), ()))
nn = (((1,), (0,)), ((), ()))


def dot(a, b, dims):
    return lax.dot_general(a, b, dims, preferred_element_type=jnp.float32)


def build_kernel(rows_ref, cols_ref, count_ref, near_ref, weight_ref, high_ref, low_ref, degree_ref):
    group, nearest, extent = near_ref.shape
    step = pl.program_id(0)

    @pl.when(step == 0)
    def _():
        degree_ref[...] = jnp.zeros_like(degree_ref)

    for member in range(group):
        slot = step * group + member
        alive = (slot < count_ref[0]).astype(jnp.float32)
        near = near_ref[member]
        weight = weight_ref[member].astype(jnp.float32) * alive
        total = weight
        for shift in range(1, nearest):
            same = pltpu.roll(near, shift, 0) == near
            total = total + jnp.where(same, pltpu.roll(weight, shift, 0), 0.0)
        high = total.astype(jnp.bfloat16)
        low = (total - high.astype(jnp.float32)).astype(jnp.bfloat16)
        near = near.astype(jnp.float32).astype(jnp.bfloat16)
        chunk = 64
        for half in range(extent // 128):
            lanes = slice(half * 128, half * 128 + 128)
            for part in range(extent // chunk):
                iota = lax.broadcasted_iota(jnp.int32, (chunk, 128), 0) + part * chunk
                iota = iota.astype(jnp.float32).astype(jnp.bfloat16)
                high_acc = jnp.zeros((chunk, 128), jnp.bfloat16)
                low_acc = jnp.zeros((chunk, 128), jnp.bfloat16)
                for k in range(nearest):
                    hit = iota == jnp.broadcast_to(near[k : k + 1, lanes], (chunk, 128))
                    high_acc = jnp.where(hit, jnp.broadcast_to(high[k : k + 1, lanes], (chunk, 128)), high_acc)
                    low_acc = jnp.where(hit, jnp.broadcast_to(low[k : k + 1, lanes], (chunk, 128)), low_acc)
                high_ref[member, part * chunk : part * chunk + chunk, lanes] = high_acc
                low_ref[member, part * chunk : part * chunk + chunk, lanes] = low_acc
        ones = jnp.ones((16, extent), jnp.bfloat16)
        col_sum = dot(ones, high_ref[member], nt) + dot(ones, low_ref[member], nt)
        row_sum = jnp.sum(weight, axis=0, keepdims=True)
        degree_ref[pl.ds(rows_ref[slot], 1), :] += row_sum
        degree_ref[pl.ds(cols_ref[slot], 1), :] += col_sum[0:1]


def split_into(target, value, start):
    columns, length = value.shape
    high = value.astype(jnp.bfloat16)
    low = (value - high.astype(jnp.float32)).astype(jnp.bfloat16)
    target[:columns, start : start + length] = high
    target[columns:, start : start + length] = low


def product(split_ref, block, high, low, dims):
    columns = split_ref.shape[0] // 2
    extent = high.shape[0]
    both = split_ref[:, pl.ds(pl.multiple_of(block * extent, extent), extent)]
    first = dot(both, high, dims)
    return first[:columns] + first[columns:] + dot(both[:columns], low, dims)


def add_block(out_ref, block, value):
    extent = value.shape[1]
    out_ref[:, pl.ds(pl.multiple_of(block * extent, extent), extent)] += value


def mirror_kernel(rows_ref, cols_ref, vector_ref, high_ref, low_ref, out_ref, split_ref):
    group = high_ref.shape[0]
    step = pl.program_id(0)

    @pl.when(step == 0)
    def _():
        out_ref[...] = jnp.zeros_like(out_ref)
        split_into(split_ref, vector_ref[...], 0)

    for member in range(group):
        slot = step * group + member
        add_block(out_ref, cols_ref[slot], product(split_ref, rows_ref[slot], high_ref[member], low_ref[member], nt))


def forward_kernel(rows_ref, cols_ref, own_ref, next_ref, later_ref, high_ref, low_ref, out_ref, split_ref):
    group = high_ref.shape[0]
    step = pl.program_id(0)

    @pl.when(step == 0)
    def _():
        out_ref[...] = jnp.zeros_like(out_ref)
        split_into(split_ref, own_ref[...], 0)
        split_into(split_ref, next_ref[...], own_ref.shape[1])
        split_into(split_ref, later_ref[...], 2 * own_ref.shape[1])

    for member in range(group):
        slot = step * group + member
        add_block(out_ref, rows_ref[slot], product(split_ref, cols_ref[slot], high_ref[member], low_ref[member], nn))


def position(index):
    across = lax.axis_size("col")
    return {"row": index // across, "col": index % across}


def place_of():
    return lax.axis_index("row") * lax.axis_size("col") + lax.axis_index("col")


def degree_exchange(devices, parts_ref, out_ref, below, further, above, beyond, send_sem, recv_sem):
    own = parts_ref.shape[0] // 3
    place = place_of()
    barrier = pltpu.get_barrier_semaphore()
    for steps in (1, 2, -1, -2):
        pl.semaphore_signal(
            barrier, inc=1, device_id=position((place + steps + devices) % devices), device_id_type=pl.DeviceIdType.MESH
        )
    pl.semaphore_wait(barrier, 4)
    plan = ((1, own, 2, below), (2, 2 * own, 1, further), (-1, 0, 2, above), (-2, 0, 1, beyond))
    copies = []
    for index, (steps, start, blocks, target) in enumerate(plan):
        copy = pltpu.make_async_remote_copy(
            src_ref=parts_ref.at[start : start + blocks * own],
            dst_ref=target,
            send_sem=send_sem.at[index],
            recv_sem=recv_sem.at[index],
            device_id=position((place + steps + devices) % devices),
            device_id_type=pl.DeviceIdType.MESH,
        )
        copy.start()
        copies.append(copy)
    for copy in copies:
        copy.wait()
    out_ref[0:own] = parts_ref[0:own] + below[0:own] + further[...]
    out_ref[own : 2 * own] = above[0:own] + parts_ref[own : 2 * own] + below[own : 2 * own]
    out_ref[2 * own :] = beyond[...] + above[own : 2 * own] + parts_ref[2 * own :]


def sum_kernel(devices, value_ref, out_ref, landed, send_sem, recv_sem):
    place = place_of()
    barrier = pltpu.get_barrier_semaphore()

    def greet(steps, unused):
        pl.semaphore_signal(
            barrier, inc=1, device_id=position((place + steps) % devices), device_id_type=pl.DeviceIdType.MESH
        )
        return unused

    def copy_to(steps):
        return pltpu.make_async_remote_copy(
            src_ref=value_ref,
            dst_ref=landed.at[steps],
            send_sem=send_sem.at[steps],
            recv_sem=recv_sem.at[steps],
            device_id=position((place + steps) % devices),
            device_id_type=pl.DeviceIdType.MESH,
        )

    def begin(steps, unused):
        copy_to(steps).start()
        return unused

    def finish(steps, unused):
        copy_to(steps).wait()
        return unused

    lax.fori_loop(1, devices, greet, 0)
    pl.semaphore_wait(barrier, devices - 1)
    lax.fori_loop(1, devices, begin, 0)
    lax.fori_loop(1, devices, finish, 0)
    out_ref[...] = lax.fori_loop(1, devices, lambda steps, total: total + landed[steps], value_ref[...])


def whole(shape):
    return pl.BlockSpec(shape, lambda i, *_: (0,) * len(shape))


def params():
    return pltpu.CompilerParams(vmem_limit_bytes=48 * 1024 * 1024)


def shards(sketch, tile_row, tile_col, tile_count, neighbors, weights):
    columns, piece = sketch.shape
    slots, nearest, extent = neighbors.shape[2:]
    own_blocks = piece // extent
    axes = ("row", "col")
    devices = lax.axis_size("row") * lax.axis_size("col")
    place = place_of()
    later_len = (own_blocks - 1 + reach - 2 * own_blocks + 1) * extent

    def moved(value, steps):
        return lax.ppermute(value, axes, [(d, d + steps) for d in range(devices) if 0 <= d + steps < devices])

    base = place * own_blocks
    rows = jnp.clip(tile_row.reshape(slots) - base, 0, own_blocks - 1)
    cols = jnp.clip(tile_col.reshape(slots) - base, 0, own_blocks - 1 + reach)
    count = tile_count.reshape(1)
    near = neighbors.reshape(slots, nearest, extent)
    weight = weights.reshape(slots, nearest, extent)
    signs = sketch.astype(jnp.float32)
    next_signs = moved(signs, -1)
    later_signs = moved(signs[:, :later_len], -2)

    def tiles(size, *tail):
        return pl.BlockSpec((size,) + tail, lambda i, *_: (i,) + (0,) * len(tail))

    high, low, parts = pl.pallas_call(
        build_kernel,
        grid_spec=pltpu.PrefetchScalarGridSpec(
            num_scalar_prefetch=3,
            grid=(slots // build_group,),
            in_specs=[tiles(build_group, nearest, extent)] * 2,
            out_specs=[tiles(build_group, extent, extent)] * 2 + [whole((3 * own_blocks, extent))],
        ),
        out_shape=[jax.ShapeDtypeStruct((slots, extent, extent), jnp.bfloat16)] * 2
        + [jax.ShapeDtypeStruct((3 * own_blocks, extent), jnp.float32)],
        compiler_params=params(),
        cost_estimate=pl.CostEstimate(flops=10**10, bytes_accessed=25 * 10**6, transcendentals=0),
        name="build",
    )(rows, cols, count, near, weight)
    vmem = pl.BlockSpec(memory_space=pltpu.VMEM)
    landing = [pltpu.VMEM((blocks * own_blocks, extent), jnp.float32) for blocks in (2, 1, 2, 1)]
    degrees = pl.pallas_call(
        functools.partial(degree_exchange, devices),
        out_shape=jax.ShapeDtypeStruct(parts.shape, jnp.float32),
        in_specs=[vmem],
        out_specs=vmem,
        scratch_shapes=landing + [pltpu.SemaphoreType.DMA((4,))] * 2,
        compiler_params=pltpu.CompilerParams(collective_id=1, has_side_effects=True),
        name="degrees",
    )(parts)
    degree, next_degree, later_degree = degrees.reshape(3, piece)
    diagonal = degree[None, :] + ridge_term
    right_side = signs * jnp.sqrt(degree)[None, :]
    next_side = next_signs * jnp.sqrt(next_degree)[None, :]
    later_side = later_signs * jnp.sqrt(later_degree)[None, :later_len]

    def mirror(vector):
        length = 2 * piece + later_len
        return pl.pallas_call(
            mirror_kernel,
            grid_spec=pltpu.PrefetchScalarGridSpec(
                num_scalar_prefetch=2,
                grid=(slots // apply_group,),
                in_specs=[whole((columns, piece))] + [tiles(apply_group, extent, extent)] * 2,
                out_specs=whole((columns, length)),
                scratch_shapes=[pltpu.VMEM((2 * columns, piece), jnp.bfloat16)],
            ),
            out_shape=jax.ShapeDtypeStruct((columns, length), jnp.float32),
            compiler_params=params(),
            cost_estimate=pl.CostEstimate(flops=5 * 10**9, bytes_accessed=20 * 10**6, transcendentals=0),
            name="mirror",
        )(rows, cols, vector, high, low)

    def forward(vector, following, later):
        return pl.pallas_call(
            forward_kernel,
            grid_spec=pltpu.PrefetchScalarGridSpec(
                num_scalar_prefetch=2,
                grid=(slots // apply_group,),
                in_specs=[whole((columns, piece)), whole((columns, piece)), whole((columns, later_len))]
                + [tiles(apply_group, extent, extent)] * 2,
                out_specs=whole((columns, piece)),
                scratch_shapes=[pltpu.VMEM((2 * columns, 2 * piece + later_len), jnp.bfloat16)],
            ),
            out_shape=jax.ShapeDtypeStruct((columns, piece), jnp.float32),
            compiler_params=params(),
            cost_estimate=pl.CostEstimate(flops=5 * 10**9, bytes_accessed=20 * 10**6, transcendentals=0),
            name="forward",
        )(rows, cols, vector, following, later, high, low)

    def operate(vector, following, later):
        outgoing = mirror(vector)
        first = moved(outgoing[:, piece : 2 * piece], 1)
        second = moved(outgoing[:, 2 * piece :], 2)
        inside = forward(vector, following, later)
        second = jnp.pad(second, ((0, 0), (0, piece - later_len)))
        return diagonal * vector - (inside + outgoing[:, :piece] + first + second)

    applied = operate(right_side, next_side, later_side)
    twice = operate(applied, moved(applied, -1), moved(applied[:, :later_len], -2))
    dots = jnp.stack(
        [
            jnp.sum(right_side * right_side, axis=1),
            jnp.sum(right_side * applied, axis=1),
            jnp.sum(applied * applied, axis=1),
            jnp.sum(applied * twice, axis=1),
        ]
    )
    dots = jnp.pad(dots, ((0, 4), (0, 128 - columns)))
    dots = pl.pallas_call(
        functools.partial(sum_kernel, devices),
        out_shape=jax.ShapeDtypeStruct(dots.shape, jnp.float32),
        in_specs=[vmem],
        out_specs=vmem,
        scratch_shapes=[pltpu.VMEM((devices,) + dots.shape, jnp.float32)] + [pltpu.SemaphoreType.DMA((devices,))] * 2,
        compiler_params=pltpu.CompilerParams(collective_id=2, has_side_effects=True),
        name="total",
    )(dots)
    norm, cross, square, triple = dots[:4, :columns]
    first_step = norm / cross
    next_norm = norm - 2.0 * first_step * cross + first_step * first_step * square
    ratio = next_norm / norm
    energy = cross - 2.0 * first_step * square + first_step * first_step * triple
    second_step = next_norm / (energy - ratio * next_norm / first_step)
    residual = right_side - first_step[:, None] * applied
    direction = residual + ratio[:, None] * right_side
    along = applied - first_step[:, None] * twice + ratio[:, None] * applied
    solution = first_step[:, None] * right_side + second_step[:, None] * direction
    residual = residual - second_step[:, None] * along
    return (solution, residual)


def solution(mesh):
    placed = (
        P(None, ("groups", "row", "col")),
        P(("groups", "row"), "col", None),
        P(("groups", "row"), "col", None),
        P(("groups", "row"), "col"),
        P(("groups", "row"), "col", None, None, None),
        P(("groups", "row"), "col", None, None, None),
    )
    return jax.shard_map(
        shards,
        mesh=mesh,
        in_specs=placed,
        out_specs=(P(None, ("groups", "row", "col")), P(None, ("groups", "row", "col"))),
        check_vma=False,
    )
```

profile of v0, /device:TPU:0, one launch (start us, length us, event | category | flops | bytes accessed | tf_op | source)
XLA Modules:
  0.0 136.7 jit_solution(13935482360469251653)
XLA Ops:
  0.6 0.0 copy-start.7
  0.6 0.0 copy-start.6
  0.7 0.0 copy-start.1
  0.7 0.0 copy-start.2
  0.7 1.2 convert_element_type.8
  1.9 1.3 collective-permute-start
  3.2 0.8 slice.48
  4.0 1.3 collective-permute-start.1
  5.9 0.0 copy-done.7
  5.9 0.0 copy-done.6
  6.0 0.0 copy-done.1
  6.0 0.0 copy-done.2
  6.0 0.0 copy-start.3
  6.0 29.5 %build.1 = (bf16[64,256,256]{2,1,0:T(8,128)(2,1)}, bf16[64,256,256]{2,1,0:T(8,128)(2,1)}, f32[24,256]{1,0:T(8,128)S(1)}) custom-call(s32[64]{0:T(128)S(1)} %get-tuple-element.23.rows_ref, s32[64]{0:T(128)S(1)} %get-tuple-element.22.cols_ref, s32[1]{0:T(128)} %bitcast.58.count_ref, s32[64,16,256]{2,1,0:T(8,128)S(1)} %bitcast.59, bf16[64,16,256]{2,1,0:T(8,128)(2,1)S(1)} %bitcast.60), custom_call_target="tpu_custom_call" | custom-call | flops 10000000000 | bytes 25000000 | tf_op jit(solution)/shard_map/build/pallas_call | solution.py:219
  35.5 0.0 copy-start
  35.5 0.6 copy-done
  36.1 12.2 %degrees.1 = f32[24,256]{1,0:T(8,128)} custom-call(f32[24,256]{1,0:T(8,128)} %copy-done), custom_call_target="tpu_custom_call" | custom-call | tf_op jit(solution)/shard_map/degrees/pallas_call | solution.py:235
  48.3 1.3 add_bitcast_fusion
  49.7 0.0 copy-done.3
  49.7 11.3 %mirror.2 = f32[64,5888]{1,0:T(8,128)S(1)} custom-call(s32[64]{0:T(128)S(1)} %get-tuple-element.23.rows_ref, s32[64]{0:T(128)S(1)} %get-tuple-element.22.cols_ref, f32[64,2048]{1,0:T(8,128)S(1)} %broadcast_multiply_fusion.1.own_ref.vector_ref, bf16[64,256,256]{2,1,0:T(8,128)(2,1)} %get-tuple-element.6.high_ref, bf16[64,256,256]{2,1,0:T(8,128)(2,1)} %get-tuple-element.7.low_ref), custom_call_target="tpu_custom_call" | custom-call | flops 5000000000 | bytes 20000000 | tf_op jit(solution)/shard_map/mirror/pallas_call | solution.py:252
  61.0 0.8 slice.51
  61.8 2.2 %collective-permute-start.2 = (f32[64,2048]{1,0:T(8,128)}, f32[64,2048]{1,0:T(8,128)}, u32[]{:S(2)}, u32[]{:S(2)}) collective-permute-start(f32[64,2048]{1,0:T(8,128)} %slice.51), channel_id=1, source_target_pairs={{0,1},{1,2},{2,3},{3,4},{4,5},{5,6},{6,7},{7,8},{8,9},{9,10},{10,1... | collective-permute-start | bytes 1572872 | tf_op jit(solution)/shard_map/ppermute | solution.py:204
  64.0 0.8 slice.52
  64.8 3.9 %collective-permute-start.3 = (f32[64,1792]{1,0:T(8,128)}, f32[64,1792]{1,0:T(8,128)}, u32[]{:S(2)}, u32[]{:S(2)}) collective-permute-start(f32[64,1792]{1,0:T(8,128)} %slice.52), channel_id=1, source_target_pairs={{0,2},{1,3},{2,4},{3,5},{4,6},{5,7},{6,8},{7,9},{8,10},{9,11},{10,... | collective-permute-start | bytes 1376264 | tf_op jit(solution)/shard_map/ppermute | solution.py:204
  68.7 0.6 slice_sqrt_fusion
  69.3 1.3 slice.40
  70.6 0.7 copy.10
  71.3 0.7 copy.9
  72.0 0.0 copy-start.5
  72.0 0.0 collective-permute-done.1
  72.0 0.7 broadcast_multiply_fusion.2.later_ref
  72.8 0.0 collective-permute-done
  72.8 1.1 broadcast_multiply_fusion.next_ref
  73.9 10.1 %forward.2 = f32[64,2048]{1,0:T(8,128)S(1)} custom-call(s32[64]{0:T(128)S(1)} %get-tuple-element.23.rows_ref, s32[64]{0:T(128)S(1)} %get-tuple-element.22.cols_ref, f32[64,2048]{1,0:T(8,128)S(1)} %broadcast_multiply_fusion.1.own_ref.vector_ref, f32[64,2048]{1,0:T(8,128)S(1)} %broadcast_multiply_fusion.next_ref, ...), custom_call_target="tpu_custom_call" | custom-call | flops 5000000000 | bytes 20000000 | tf_op jit(solution)/shard_map/forward/pallas_call | solution.py:268
  84.0 0.0 collective-permute-done.3
  84.0 0.0 collective-permute-done.2
  84.0 1.3 fusion.5.own_ref.vector_ref
  85.4 1.3 collective-permute-start.4
  86.7 1.3 collective-permute-start.5
  88.0 11.3 %mirror.3 = f32[64,5888]{1,0:T(8,128)S(1)} custom-call(s32[64]{0:T(128)S(1)} %get-tuple-element.23.rows_ref, s32[64]{0:T(128)S(1)} %get-tuple-element.22.cols_ref, f32[64,2048]{1,0:T(8,128)S(1)} %fusion.5.own_ref.vector_ref, bf16[64,256,256]{2,1,0:T(8,128)(2,1)} %get-tuple-element.6.high_ref, bf16[64,256,256]{2,1,0:T(8,128)(2,1)} %get-tuple-element.7.low_ref), custom_call_target="tpu_custom_call" | custom-call | flops 5000000000 | bytes 20000000 | tf_op jit(solution)/shard_map/mirror/pallas_call | solution.py:252
  99.3 3.1 %collective-permute-start.6 = (f32[64,2048]{1,0:T(8,128)S(1)}, f32[64,2048]{1,0:T(8,128)S(1)}, u32[]{:S(2)}, u32[]{:S(2)}) collective-permute-start(f32[64,2048]{1,0:T(8,128)S(1)} %slice.55), channel_id=1, source_target_pairs={{0,1},{1,2},{2,3},{3,4},{4,5},{5,6},{6,7},{7,8},{8,9},{9,10},{10,1... | collective-permute-start | bytes 1572872 | tf_op jit(solution)/shard_map/ppermute | solution.py:204
  102.4 4.3 %collective-permute-start.7 = (f32[64,1792]{1,0:T(8,128)S(1)}, f32[64,1792]{1,0:T(8,128)S(1)}, u32[]{:S(2)}, u32[]{:S(2)}) collective-permute-start(f32[64,1792]{1,0:T(8,128)S(1)} %slice.56), channel_id=1, source_target_pairs={{0,2},{1,3},{2,4},{3,5},{4,6},{5,7},{6,8},{7,9},{8,10},{9,11},{10,... | collective-permute-start | bytes 1376264 | tf_op jit(solution)/shard_map/ppermute | solution.py:204
  106.7 0.0 collective-permute-done.5.later_ref
  106.7 0.0 collective-permute-done.4.next_ref
  106.7 10.1 %forward.3 = f32[64,2048]{1,0:T(8,128)S(1)} custom-call(s32[64]{0:T(128)S(1)} %get-tuple-element.23.rows_ref, s32[64]{0:T(128)S(1)} %get-tuple-element.22.cols_ref, f32[64,2048]{1,0:T(8,128)S(1)} %fusion.5.own_ref.vector_ref, f32[64,2048]{1,0:T(8,128)S(1)} %collective-permute-done.4.next_ref, f32[64,1792]{1,0:T(8,128)S(1)} %collective-permute-done.5.later_ref, ...), custom_call_target="tpu_custom_call" | custom-call | flops 5000000000 | bytes 20000000 | tf_op jit(solution)/shard_map/forward/pallas_call | solution.py:268
  116.8 0.8 collective-permute-done.7
  117.6 0.0 collective-permute-done.6
  117.6 0.0 copy-done.5
  117.6 0.0 copy-start.4
  117.6 0.4 multiply_reduce_fusion.3
  118.0 0.4 copy-done.4
  118.4 0.6 select_maximum_fusion.value_ref
  119.0 13.7 %total.1 = f32[8,128]{1,0:T(8,128)} custom-call(f32[8,128]{1,0:T(8,128)} %select_maximum_fusion.value_ref), custom_call_target="tpu_custom_call" | custom-call | tf_op jit(solution)/shard_map/total/pallas_call | solution.py:303
  132.7 0.8 fusion.9
  133.5 0.8 fusion.8
  134.3 2.4 %multiply_subtract_fusion = (f32[64,2048]{1,0:T(8,128)}, f32[64,2048]{1,0:T(8,128)}) fusion(f32[64,2048]{1,0:T(8,128)S(1)} %fusion.5.own_ref.vector_ref, f32[64]{0:T(128)S(1)} %get-tuple-element.13, f32[64]{0:T(128)S(1)} %get-tuple-element.12, f32[64]{0:T(128)S(1)} %get-tuple-element.15, f32[64,1792]{1,0:T(8,128)S(1)} %collective-permute-done.7, ...), kind=kLoop, calls=%fused_computation.8 | loop fusion | flops 2621440 | bytes 4145920 | tf_op jit(solution)/shard_map/sub | solution.py:322
  (6 shorter events, 0.2 us)
Async XLA Ops:
  0.6 5.3 %copy-start.7 = (s32[1,1,64]{2,1,0:T(1,128)S(1)}, s32[1,1,64]{2,1,0:T(1,128)}, u32[]{:S(2)}) copy-start(s32[1,1,64]{2,1,0:T(1,128)} %param.7) | copy-start | bytes 772
  0.6 5.3 %copy-start.6 = (s32[1,1,64]{2,1,0:T(1,128)S(1)}, s32[1,1,64]{2,1,0:T(1,128)}, u32[]{:S(2)}) copy-start(s32[1,1,64]{2,1,0:T(1,128)} %param.8) | copy-start | bytes 772
  0.7 5.3 %copy-start.1 = (s32[1,1,64,16,256]{4,3,2,1,0:T(8,128)S(1)}, s32[1,1,64,16,256]{4,3,2,1,0:T(8,128)}, u32[]{:S(2)}) copy-start(s32[1,1,64,16,256]{4,3,2,1,0:T(8,128)} %param.10) | copy-start | bytes 3145732
  0.7 5.3 %copy-start.2 = (bf16[1,1,64,16,256]{4,3,2,1,0:T(8,128)(2,1)S(1)}, bf16[1,1,64,16,256]{4,3,2,1,0:T(8,128)(2,1)}, u32[]{:S(2)}) copy-start(bf16[1,1,64,16,256]{4,3,2,1,0:T(8,128)(2,1)} %param.11) | copy-start | bytes 1572868
  1.9 70.9 %collective-permute-start = (f32[64,2048]{1,0:T(8,128)S(1)}, f32[64,2048]{1,0:T(8,128)}, u32[]{:S(2)}, u32[]{:S(2)}) collective-permute-start(f32[64,2048]{1,0:T(8,128)S(1)} %convert_element_type.8), channel_id=1, source_target_pairs={{1,0},{2,1},{3,2},{4,3},{5,4},{6,5},{7,6},{8,7},{9,8},{10,9},{11,1... | collective-permute-start | bytes 1572872 | tf_op jit(solution)/shard_map/ppermute | solution.py:204
  4.0 68.0 %collective-permute-start.1 = (f32[64,1792]{1,0:T(8,128)}, f32[64,1792]{1,0:T(8,128)S(1)}, u32[]{:S(2)}, u32[]{:S(2)}) collective-permute-start(f32[64,1792]{1,0:T(8,128)} %slice.48), channel_id=1, source_target_pairs={{2,0},{3,1},{4,2},{5,3},{6,4},{7,5},{8,6},{9,7},{10,8},{11,9},{12,... | collective-permute-start | bytes 1376264 | tf_op jit(solution)/shard_map/ppermute | solution.py:204
  6.0 43.7 %copy-start.3 = (s32[64,2048]{1,0:T(8,128)S(1)}, s32[64,2048]{1,0:T(8,128)}, u32[]{:S(2)}) copy-start(s32[64,2048]{1,0:T(8,128)} %param.6) | copy-start | bytes 1572868
  35.5 0.6 copy-start
  61.8 22.2 %collective-permute-start.2 = (f32[64,2048]{1,0:T(8,128)}, f32[64,2048]{1,0:T(8,128)}, u32[]{:S(2)}, u32[]{:S(2)}) collective-permute-start(f32[64,2048]{1,0:T(8,128)} %slice.51), channel_id=1, source_target_pairs={{0,1},{1,2},{2,3},{3,4},{4,5},{5,6},{6,7},{7,8},{8,9},{9,10},{10,1... | collective-permute-start | bytes 1572872 | tf_op jit(solution)/shard_map/ppermute | solution.py:204
  64.8 19.2 %collective-permute-start.3 = (f32[64,1792]{1,0:T(8,128)}, f32[64,1792]{1,0:T(8,128)}, u32[]{:S(2)}, u32[]{:S(2)}) collective-permute-start(f32[64,1792]{1,0:T(8,128)} %slice.52), channel_id=1, source_target_pairs={{0,2},{1,3},{2,4},{3,5},{4,6},{5,7},{6,8},{7,9},{8,10},{9,11},{10,... | collective-permute-start | bytes 1376264 | tf_op jit(solution)/shard_map/ppermute | solution.py:204
  72.0 45.6 %copy-start.5 = (f32[1,2,8,128]{3,1,2,0:T(2,128)}, f32[1,2,8,128]{3,1,2,0:T(2,128)S(1)}, u32[]{:S(2)}) copy-start(f32[1,2,8,128]{3,1,2,0:T(2,128)S(1)} %copy.9) | copy-start | bytes 24580
  85.4 21.3 %collective-permute-start.4 = (f32[64,2048]{1,0:T(8,128)S(1)}, f32[64,2048]{1,0:T(8,128)S(1)}, u32[]{:S(2)}, u32[]{:S(2)}) collective-permute-start(f32[64,2048]{1,0:T(8,128)S(1)} %fusion.5.own_ref.vector_ref), channel_id=1, source_target_pairs={{1,0},{2,1},{3,2},{4,3},{5,4},{6,5},{7,6},{8,7},{9,8},{10,9},{11,1... | collective-permute-start | bytes 1572872 | tf_op jit(solution)/shard_map/ppermute | solution.py:204
  86.7 20.0 %collective-permute-start.5 = (f32[64,1792]{1,0:T(8,128)S(1)}, f32[64,1792]{1,0:T(8,128)S(1)}, u32[]{:S(2)}, u32[]{:S(2)}) collective-permute-start(f32[64,1792]{1,0:T(8,128)S(1)} %slice.53), channel_id=1, source_target_pairs={{2,0},{3,1},{4,2},{5,3},{6,4},{7,5},{8,6},{9,7},{10,8},{11,9},{12,... | collective-permute-start | bytes 1376264 | tf_op jit(solution)/shard_map/ppermute | solution.py:204
  99.3 18.3 %collective-permute-start.6 = (f32[64,2048]{1,0:T(8,128)S(1)}, f32[64,2048]{1,0:T(8,128)S(1)}, u32[]{:S(2)}, u32[]{:S(2)}) collective-permute-start(f32[64,2048]{1,0:T(8,128)S(1)} %slice.55), channel_id=1, source_target_pairs={{0,1},{1,2},{2,3},{3,4},{4,5},{5,6},{6,7},{7,8},{8,9},{9,10},{10,1... | collective-permute-start | bytes 1572872 | tf_op jit(solution)/shard_map/ppermute | solution.py:204
  102.4 15.2 %collective-permute-start.7 = (f32[64,1792]{1,0:T(8,128)S(1)}, f32[64,1792]{1,0:T(8,128)S(1)}, u32[]{:S(2)}, u32[]{:S(2)}) collective-permute-start(f32[64,1792]{1,0:T(8,128)S(1)} %slice.56), channel_id=1, source_target_pairs={{0,2},{1,3},{2,4},{3,5},{4,6},{5,7},{6,8},{7,9},{8,10},{9,11},{10,... | collective-permute-start | bytes 1376264 | tf_op jit(solution)/shard_map/ppermute | solution.py:204
  117.6 0.8 copy-start.4
where the time goes:
time: 138 us; the launch traced here: 137 us
  Pallas kernels  98.1 us (71%)
  starting transfers between devices  18.6 us (13%)
  other arithmetic  10.8 us (8%)
  local copies, waits for them, and re-layouts  6.86 us (5%)
  between operations  1.57 us (1%)
    pallas_call x1, Pallas kernels, shards(): pl.pallas_call(build_kernel, grid_spec=pltpu.PrefetchScalarGridSpec(num_s...  29.5 us
    pallas_call x2, Pallas kernels, mirror(): pl.pallas_call(mirror_kernel, grid_spec=pltpu.PrefetchScalarGridSpec(num_...  22.5 us
    pallas_call x2, Pallas kernels, forward(): pl.pallas_call(forward_kernel, grid_spec=pltpu.PrefetchScalarGridSpec(num...  20.2 us
    ppermute x8, starting transfers between devices, moved(): lax.ppermute(value, axes, [(d, d + steps) for d in range(devices) if 0 <=...  18.6 us
    pallas_call x1, Pallas kernels, shards(): pl.pallas_call(functools.partial(sum_kernel, devices), out_shape=jax.Shap...  13.7 us
    pallas_call x1, Pallas kernels, shards(): pl.pallas_call(functools.partial(degree_exchange, devices), out_shape=jax...  12.2 us
  transfers between devices with their start and end apart: 8, of which 1 were waited for; matrix products, arithmetic and copies ran while one was open for 7% of the time, Pallas kernels for 62%

commit v1 on v0

--- a/solution.py
+++ b/solution.py
@@ -7,8 +7,9 @@
 from jax.sharding import PartitionSpec as P
 
 ridge_term = 1.0
-build_group = 4
-apply_group = 8
+build_group = 16
+unrolled = 4
+apply_group = 16
 reach = 15
 nt = (((1,), (1,)), ((), ()))
 nn = (((1,), (0,)), ((), ()))
@@ -26,9 +27,8 @@
     def _():
         degree_ref[...] = jnp.zeros_like(degree_ref)
 
-    for member in range(group):
-        slot = step * group + member
-        alive = (slot < count_ref[0]).astype(jnp.float32)
+    def visit(member):
+        alive = (step * group + member < count_ref[0]).astype(jnp.float32)
         near = near_ref[member]
         weight = weight_ref[member].astype(jnp.float32) * alive
         total = weight
@@ -52,11 +52,23 @@
                     low_acc = jnp.where(hit, jnp.broadcast_to(low[k : k + 1, lanes], (chunk, 128)), low_acc)
                 high_ref[member, part * chunk : part * chunk + chunk, lanes] = high_acc
                 low_ref[member, part * chunk : part * chunk + chunk, lanes] = low_acc
+        return jnp.sum(weight, axis=0, keepdims=True)
+
+    def add_degree(member, row_sum):
+        slot = step * group + member
         ones = jnp.ones((16, extent), jnp.bfloat16)
         col_sum = dot(ones, high_ref[member], nt) + dot(ones, low_ref[member], nt)
-        row_sum = jnp.sum(weight, axis=0, keepdims=True)
         degree_ref[pl.ds(rows_ref[slot], 1), :] += row_sum
         degree_ref[pl.ds(cols_ref[slot], 1), :] += col_sum[0:1]
+
+    @pl.loop(0, group // unrolled)
+    def _(turn):
+        row_sums = []
+        for member in range(unrolled):
+            row_sums.append(visit(turn * unrolled + member))
+            if member > 0:
+                add_degree(turn * unrolled + member - 1, row_sums[member - 1])
+        add_degree(turn * unrolled + unrolled - 1, row_sums[-1])
 
 
 def split_into(target, value, start):
@@ -80,9 +92,10 @@
     out_ref[:, pl.ds(pl.multiple_of(block * extent, extent), extent)] += value
 
 
-def mirror_kernel(rows_ref, cols_ref, vector_ref, high_ref, low_ref, out_ref, split_ref):
+def mirror_kernel(rows_ref, cols_ref, vector_ref, high_ref, low_ref, own_ref, next_ref, later_ref, out_ref, split_ref):
     group = high_ref.shape[0]
     step = pl.program_id(0)
+    piece = own_ref.shape[1]
 
     @pl.when(step == 0)
     def _():
@@ -92,6 +105,12 @@
     for member in range(group):
         slot = step * group + member
         add_block(out_ref, cols_ref[slot], product(split_ref, rows_ref[slot], high_ref[member], low_ref[member], nt))
+
+    @pl.when(step == pl.num_programs(0) - 1)
+    def _():
+        own_ref[...] = out_ref[:, :piece]
+        next_ref[...] = out_ref[:, piece : 2 * piece]
+        later_ref[...] = out_ref[:, 2 * piece :]
 
 
 def forward_kernel(rows_ref, cols_ref, own_ref, next_ref, later_ref, high_ref, low_ref, out_ref, split_ref):
@@ -248,17 +267,20 @@
     later_side = later_signs * jnp.sqrt(later_degree)[None, :later_len]
 
     def mirror(vector):
-        length = 2 * piece + later_len
+        lengths = (piece, piece, later_len)
         return pl.pallas_call(
             mirror_kernel,
             grid_spec=pltpu.PrefetchScalarGridSpec(
                 num_scalar_prefetch=2,
                 grid=(slots // apply_group,),
                 in_specs=[whole((columns, piece))] + [tiles(apply_group, extent, extent)] * 2,
-                out_specs=whole((columns, length)),
-                scratch_shapes=[pltpu.VMEM((2 * columns, piece), jnp.bfloat16)],
+                out_specs=[whole((columns, length)) for length in lengths],
+                scratch_shapes=[
+                    pltpu.VMEM((columns, sum(lengths)), jnp.float32),
+                    pltpu.VMEM((2 * columns, piece), jnp.bfloat16),
+                ],
             ),
-            out_shape=jax.ShapeDtypeStruct((columns, length), jnp.float32),
+            out_shape=[jax.ShapeDtypeStruct((columns, length), jnp.float32) for length in lengths],
             compiler_params=params(),
             cost_estimate=pl.CostEstimate(flops=5 * 10**9, bytes_accessed=20 * 10**6, transcendentals=0),
             name="mirror",
@@ -282,12 +304,12 @@
         )(rows, cols, vector, following, later, high, low)
 
     def operate(vector, following, later):
-        outgoing = mirror(vector)
-        first = moved(outgoing[:, piece : 2 * piece], 1)
-        second = moved(outgoing[:, 2 * piece :], 2)
+        kept, first, second = mirror(vector)
+        first = moved(first, 1)
+        second = moved(second, 2)
         inside = forward(vector, following, later)
         second = jnp.pad(second, ((0, 0), (0, piece - later_len)))
-        return diagonal * vector - (inside + outgoing[:, :piece] + first + second)
+        return diagonal * vector - (inside + kept + first + second)
 
     applied = operate(right_side, next_side, later_side)
     twice = operate(applied, moved(applied, -1), moved(applied[:, :later_len], -2))

time: 138 us -> 134 us (0.971)
  Pallas kernels: 98.1 us -> 93.8 us
  waiting for transfers between devices: 0.83 us -> 2.44 us
    pallas_call x2, Pallas kernels: 20.2 us -> 16.9 us  [forward(): pl.pallas_call(forward_kernel, grid_spec=pltpu.PrefetchScalarGridSpec(num...]
    pallas_call x2, Pallas kernels: 22.5 us -> 19.5 us  [mirror(): pl.pallas_call(mirror_kernel, grid_spec=pltpu.PrefetchScalarGridSpec(num_...]
    unnamed x19 -> x13, local copies, waits for them, and re-layouts: 2.45 us -> 4.19 us
    slice x4 -> x0, local copies, waits for them, and re-layouts: 1.69 us -> none  [the longest x2 0.86 us: operate(): first = moved(outgoing[:, piece:2 * piece], 1)]
    ppermute x8, waiting for transfers between devices: 0.83 us -> 2.44 us  [moved(): lax.ppermute(value, axes, [(d, d + steps) for d in range(devices) if 0 <=...]
  transfers between devices with their start and end apart: 8 -> 8, of which waited for: 1 -> 1; matrix products, arithmetic and copies ran while one was open for 7% -> 6% of each run, Pallas kernels for 62% -> 59%
where the time goes in v1:
time: 134 us
  Pallas kernels  93.8 us (70%)
  starting transfers between devices  18.7 us (14%)
  other arithmetic  10.3 us (8%)
  local copies, waits for them, and re-layouts  6.91 us (5%)
  waiting for transfers between devices  2.44 us (2%)
  between operations  1.48 us (1%)
    pallas_call x1, Pallas kernels, shards(): pl.pallas_call(build_kernel, grid_spec=pltpu.PrefetchScalarGridSpec(num_s...  30.7 us
    pallas_call x2, Pallas kernels, mirror(): pl.pallas_call(mirror_kernel, grid_spec=pltpu.PrefetchScalarGridSpec(num_...  19.5 us
    ppermute x8, starting transfers between devices, moved(): lax.ppermute(value, axes, [(d, d + steps) for d in range(devices) if 0 <=...  18.7 us
    pallas_call x2, Pallas kernels, forward(): pl.pallas_call(forward_kernel, grid_spec=pltpu.PrefetchScalarGridSpec(num...  16.9 us
    pallas_call x1, Pallas kernels, shards(): pl.pallas_call(functools.partial(sum_kernel, devices), out_shape=jax.Shap...  14.5 us
    pallas_call x1, Pallas kernels, shards(): pl.pallas_call(functools.partial(degree_exchange, devices), out_shape=jax...  12.2 us
    unnamed x13, local copies, waits for them, and re-layouts  4.19 us
  transfers between devices with their start and end apart: 8, of which 1 were waited for; matrix products, arithmetic and copies ran while one was open for 6% of the time, Pallas kernels for 59%

profile of v1, /device:TPU:0, one launch (start us, length us, event | category | flops | bytes accessed | tf_op | source)
XLA Modules:
  0.0 133.6 jit_solution(5458925504260654276)
XLA Ops:
  0.6 1.1 convert_element_type.8
  1.7 1.3 collective-permute-start
  3.0 0.8 slice.24
  3.8 1.3 collective-permute-start.1
  5.8 0.7 clamp_bitcast_fusion
  6.4 0.0 copy-start.1
  6.4 1.2 copy-done.1
  7.7 0.0 copy-start.2
  7.7 1.0 copy-done.2
  8.7 0.0 copy-start.3
  8.7 30.7 %build.1 = (bf16[64,256,256]{2,1,0:T(8,128)(2,1)}, bf16[64,256,256]{2,1,0:T(8,128)(2,1)}, f32[24,256]{1,0:T(8,128)S(1)}) custom-call(s32[64]{0:T(128)S(1)} %get-tuple-element.35.rows_ref, s32[64]{0:T(128)S(1)} %get-tuple-element.34.cols_ref, s32[1]{0:T(128)} %bitcast.58.count_ref, s32[64,16,256]{2,1,0:T(8,128)S(1)} %bitcast.59, bf16[64,16,256]{2,1,0:T(8,128)(2,1)S(1)} %bitcast.60), custom_call_target="tpu_custom_call" | custom-call | flops 10000000000 | bytes 25000000 | tf_op jit(solution)/shard_map/build/pallas_call | solution.py:238
  39.4 0.0 copy-start
  39.4 0.6 copy-done
  40.0 12.2 %degrees.1 = f32[24,256]{1,0:T(8,128)} custom-call(f32[24,256]{1,0:T(8,128)} %copy-done), custom_call_target="tpu_custom_call" | custom-call | tf_op jit(solution)/shard_map/degrees/pallas_call | solution.py:254
  52.1 1.3 %add_bitcast_fusion = (f32[1,2,8,128]{3,2,1,0:T(8,128)S(1)}, f32[8,256]{1,0:T(8,128)S(1)}, f32[1,2,8,128]{3,2,1,0:T(8,128)}, f32[1,2,8,128]{3,2,1,0:T(8,128)S(1)}) fusion(f32[24,256]{1,0:T(8,128)} %degrees.1), kind=kLoop, calls=%fused_computation.14 | loop fusion | flops 2048 | bytes 57344
  53.5 0.0 copy-done.3
  53.5 9.8 %mirror.2 = (f32[64,2048]{1,0:T(8,128)S(1)}, f32[64,2048]{1,0:T(8,128)S(1)}, f32[64,1792]{1,0:T(8,128)S(1)}) custom-call(s32[64]{0:T(128)S(1)} %get-tuple-element.35.rows_ref, s32[64]{0:T(128)S(1)} %get-tuple-element.34.cols_ref, f32[64,2048]{1,0:T(8,128)S(1)} %broadcast_multiply_fusion.1.own_ref.vector_ref, ...), custom_call_target="tpu_custom_call" | custom-call | flops 5000000000 | bytes 20000000 | tf_op jit(solution)/shard_map/mirror/pallas_call | solution.py:271
  63.3 4.2 %collective-permute-start.3 = (f32[64,1792]{1,0:T(8,128)S(1)}, f32[64,1792]{1,0:T(8,128)}, u32[]{:S(2)}, u32[]{:S(2)}) collective-permute-start(f32[64,1792]{1,0:T(8,128)S(1)} %get-tuple-element.16), channel_id=1, source_target_pairs={{0,2},{1,3},{2,4},{3,5},{4,6},{5,7},{6,8},{7,9},{8,10},{9,11},{10,... | collective-permute-start | bytes 1376264 | tf_op jit(solution)/shard_map/ppermute | solution.py:223
  67.5 2.1 %collective-permute-start.2 = (f32[64,2048]{1,0:T(8,128)S(1)}, f32[64,2048]{1,0:T(8,128)}, u32[]{:S(2)}, u32[]{:S(2)}) collective-permute-start(f32[64,2048]{1,0:T(8,128)S(1)} %get-tuple-element.15), channel_id=1, source_target_pairs={{0,1},{1,2},{2,3},{3,4},{4,5},{5,6},{6,7},{7,8},{8,9},{9,10},{10,1... | collective-permute-start | bytes 1572872 | tf_op jit(solution)/shard_map/ppermute | solution.py:223
  69.5 0.6 slice_sqrt_fusion
  70.1 0.6 copy.9
  70.8 1.3 slice.22
  72.0 0.7 copy.10
  72.7 0.0 collective-permute-done.1
  72.7 0.7 broadcast_multiply_fusion.2.later_ref
  73.5 0.0 collective-permute-done
  73.5 1.1 broadcast_multiply_fusion.next_ref
  74.6 0.0 copy-start.4
  74.6 8.5 %forward.2 = f32[64,2048]{1,0:T(8,128)S(1)} custom-call(s32[64]{0:T(128)S(1)} %get-tuple-element.35.rows_ref, s32[64]{0:T(128)S(1)} %get-tuple-element.34.cols_ref, f32[64,2048]{1,0:T(8,128)S(1)} %broadcast_multiply_fusion.1.own_ref.vector_ref, f32[64,2048]{1,0:T(8,128)S(1)} %broadcast_multiply_fusion.next_ref, ...), custom_call_target="tpu_custom_call" | custom-call | flops 5000000000 | bytes 20000000 | tf_op jit(solution)/shard_map/forward/pallas_call | solution.py:290
  83.1 0.0 collective-permute-done.3
  83.1 0.0 collective-permute-done.2
  83.1 0.0 copy-done.4
  83.1 1.3 %add_subtract_fusion.1.own_ref.vector_ref = f32[64,2048]{1,0:T(8,128)S(1)} fusion(f32[64,1792]{1,0:T(8,128)} %collective-permute-done.3, f32[64,2048]{1,0:T(8,128)} %collective-permute-done.2, f32[64,2048]{1,0:T(8,128)S(1)} %forward.2, f32[64,2048]{1,0:T(8,128)S(1)} %get-tuple-element.14, f32[2048]{0:T(1024)S(1)} %bitcast.65, f32[2048]{0:T(1024)S(1)} %bitcast.62, ...), kind=kLoop, calls=%fused_computation.7 | loop fusion | flops 917504 | bytes 3096576 | tf_op jit(solution)/shard_map/sub | solution.py:312
  84.5 1.3 collective-permute-start.4
  85.8 1.3 collective-permute-start.5
  87.1 9.8 %mirror.3 = (f32[64,2048]{1,0:T(8,128)S(1)}, f32[64,2048]{1,0:T(8,128)S(1)}, f32[64,1792]{1,0:T(8,128)S(1)}) custom-call(s32[64]{0:T(128)S(1)} %get-tuple-element.35.rows_ref, s32[64]{0:T(128)S(1)} %get-tuple-element.34.cols_ref, f32[64,2048]{1,0:T(8,128)S(1)} %add_subtract_fusion.1.own_ref.vector_ref, bf16[64,256,256]{2,1,0:T(8,128)(2,1)} %get-tuple-element.12.high_ref, ...), custom_call_target="tpu_custom_call" | custom-call | flops 5000000000 | bytes 20000000 | tf_op jit(solution)/shard_map/mirror/pallas_call | solution.py:271
  96.8 3.0 %collective-permute-start.6 = (f32[64,2048]{1,0:T(8,128)S(1)}, f32[64,2048]{1,0:T(8,128)S(1)}, u32[]{:S(2)}, u32[]{:S(2)}) collective-permute-start(f32[64,2048]{1,0:T(8,128)S(1)} %get-tuple-element.18), channel_id=1, source_target_pairs={{0,1},{1,2},{2,3},{3,4},{4,5},{5,6},{6,7},{7,8},{8,9},{9,10},{10,1... | collective-permute-start | bytes 1572872 | tf_op jit(solution)/shard_map/ppermute | solution.py:223
  99.9 4.3 %collective-permute-start.7 = (f32[64,1792]{1,0:T(8,128)S(1)}, f32[64,1792]{1,0:T(8,128)S(1)}, u32[]{:S(2)}, u32[]{:S(2)}) collective-permute-start(f32[64,1792]{1,0:T(8,128)S(1)} %get-tuple-element.19), channel_id=1, source_target_pairs={{0,2},{1,3},{2,4},{3,5},{4,6},{5,7},{6,8},{7,9},{8,10},{9,11},{10,... | collective-permute-start | bytes 1376264 | tf_op jit(solution)/shard_map/ppermute | solution.py:223
  104.2 0.0 collective-permute-done.5.later_ref
  104.2 0.0 collective-permute-done.4.next_ref
  104.2 8.5 %forward.3 = f32[64,2048]{1,0:T(8,128)S(1)} custom-call(s32[64]{0:T(128)S(1)} %get-tuple-element.35.rows_ref, s32[64]{0:T(128)S(1)} %get-tuple-element.34.cols_ref, f32[64,2048]{1,0:T(8,128)S(1)} %add_subtract_fusion.1.own_ref.vector_ref, f32[64,2048]{1,0:T(8,128)S(1)} %collective-permute-done.4.next_ref, f32[64,1792]{1,0:T(8,128)S(1)} %collective-permute-done.5.later_ref, ...), custom_call_target="tpu_custom_call" | custom-call | flops 5000000000 | bytes 20000000 | tf_op jit(solution)/shard_map/forward/pallas_call | solution.py:290
  112.7 2.4 %collective-permute-done.7 = f32[64,1792]{1,0:T(8,128)S(1)} collective-permute-done((f32[64,1792]{1,0:T(8,128)S(1)}, f32[64,1792]{1,0:T(8,128)S(1)}, u32[]{:S(2)}, u32[]{:S(2)}) %collective-permute-start.7) | collective-permute-done | bytes 458784 | tf_op jit(solution)/shard_map/ppermute | solution.py:223
  115.1 0.0 collective-permute-done.6
  115.1 0.4 multiply_reduce_fusion.3
  115.5 0.6 select_maximum_fusion.value_ref
  116.1 14.5 %total.1 = f32[8,128]{1,0:T(8,128)} custom-call(f32[8,128]{1,0:T(8,128)} %select_maximum_fusion.value_ref), custom_call_target="tpu_custom_call" | custom-call | tf_op jit(solution)/shard_map/total/pallas_call | solution.py:325
  130.6 0.8 fusion.3
  131.4 0.8 fusion.2
  132.3 1.4 %multiply_subtract_fusion = (f32[64,2048]{1,0:T(8,128)}, f32[64,2048]{1,0:T(8,128)}) fusion(f32[64,2048]{1,0:T(8,128)S(1)} %add_subtract_fusion.1.own_ref.vector_ref, f32[64]{0:T(128)S(1)} %get-tuple-element.25, f32[64]{0:T(128)S(1)} %get-tuple-element.24, f32[64]{0:T(128)S(1)} %get-tuple-element.27, f32[64,1792]{1,0:T(8,128)S(1)} %collective-permute-done.7, ...), kind=kLoop, calls=%fused_computation | loop fusion | flops 2621440 | bytes 4145920 | tf_op jit(solution)/shard_map/sub | solution.py:344
  (3 shorter events, 0.1 us)
Async XLA Ops:
  1.7 71.8 %collective-permute-start = (f32[64,2048]{1,0:T(8,128)S(1)}, f32[64,2048]{1,0:T(8,128)}, u32[]{:S(2)}, u32[]{:S(2)}) collective-permute-start(f32[64,2048]{1,0:T(8,128)S(1)} %convert_element_type.8), channel_id=1, source_target_pairs={{1,0},{2,1},{3,2},{4,3},{5,4},{6,5},{7,6},{8,7},{9,8},{10,9},{11,1... | collective-permute-start | bytes 1572872 | tf_op jit(solution)/shard_map/ppermute | solution.py:223
  3.8 68.9 %collective-permute-start.1 = (f32[64,1792]{1,0:T(8,128)}, f32[64,1792]{1,0:T(8,128)S(1)}, u32[]{:S(2)}, u32[]{:S(2)}) collective-permute-start(f32[64,1792]{1,0:T(8,128)} %slice.24), channel_id=1, source_target_pairs={{2,0},{3,1},{4,2},{5,3},{6,4},{7,5},{8,6},{9,7},{10,8},{11,9},{12,... | collective-permute-start | bytes 1376264 | tf_op jit(solution)/shard_map/ppermute | solution.py:223
  6.4 1.2 copy-start.1
  7.7 1.0 copy-start.2
  8.7 44.8 %copy-start.3 = (s32[64,2048]{1,0:T(8,128)S(1)}, s32[64,2048]{1,0:T(8,128)}, u32[]{:S(2)}) copy-start(s32[64,2048]{1,0:T(8,128)} %param.6) | copy-start | bytes 1572868
  39.4 0.6 copy-start
  63.3 19.7 %collective-permute-start.3 = (f32[64,1792]{1,0:T(8,128)S(1)}, f32[64,1792]{1,0:T(8,128)}, u32[]{:S(2)}, u32[]{:S(2)}) collective-permute-start(f32[64,1792]{1,0:T(8,128)S(1)} %get-tuple-element.16), channel_id=1, source_target_pairs={{0,2},{1,3},{2,4},{3,5},{4,6},{5,7},{6,8},{7,9},{8,10},{9,11},{10,... | collective-permute-start | bytes 1376264 | tf_op jit(solution)/shard_map/ppermute | solution.py:223
  67.5 15.6 %collective-permute-start.2 = (f32[64,2048]{1,0:T(8,128)S(1)}, f32[64,2048]{1,0:T(8,128)}, u32[]{:S(2)}, u32[]{:S(2)}) collective-permute-start(f32[64,2048]{1,0:T(8,128)S(1)} %get-tuple-element.15), channel_id=1, source_target_pairs={{0,1},{1,2},{2,3},{3,4},{4,5},{5,6},{6,7},{7,8},{8,9},{9,10},{10,1... | collective-permute-start | bytes 1572872 | tf_op jit(solution)/shard_map/ppermute | solution.py:223
  74.6 8.5 %copy-start.4 = (f32[1,2,8,128]{3,1,2,0:T(2,128)S(1)}, f32[1,2,8,128]{3,1,2,0:T(2,128)}, u32[]{:S(2)}) copy-start(f32[1,2,8,128]{3,1,2,0:T(2,128)} %copy.9) | copy-start | bytes 24580
  84.5 19.7 %collective-permute-start.4 = (f32[64,2048]{1,0:T(8,128)S(1)}, f32[64,2048]{1,0:T(8,128)S(1)}, u32[]{:S(2)}, u32[]{:S(2)}) collective-permute-start(f32[64,2048]{1,0:T(8,128)S(1)} %add_subtract_fusion.1.own_ref.vector_ref), channel_id=1, source_target_pairs={{1,0},{2,1},{3,2},{4,3},{5,4},{6,5},{7,6},{8,7},{9,8},{10,9},{11,1... | collective-permute-start | bytes 1572872 | tf_op jit(solution)/shard_map/ppermute | solution.py:223
  85.8 18.4 %collective-permute-start.5 = (f32[64,1792]{1,0:T(8,128)S(1)}, f32[64,1792]{1,0:T(8,128)S(1)}, u32[]{:S(2)}, u32[]{:S(2)}) collective-permute-start(f32[64,1792]{1,0:T(8,128)S(1)} %slice.26), channel_id=1, source_target_pairs={{2,0},{3,1},{4,2},{5,3},{6,4},{7,5},{8,6},{9,7},{10,8},{11,9},{12,... | collective-permute-start | bytes 1376264 | tf_op jit(solution)/shard_map/ppermute | solution.py:223
  96.8 18.3 %collective-permute-start.6 = (f32[64,2048]{1,0:T(8,128)S(1)}, f32[64,2048]{1,0:T(8,128)S(1)}, u32[]{:S(2)}, u32[]{:S(2)}) collective-permute-start(f32[64,2048]{1,0:T(8,128)S(1)} %get-tuple-element.18), channel_id=1, source_target_pairs={{0,1},{1,2},{2,3},{3,4},{4,5},{5,6},{6,7},{7,8},{8,9},{9,10},{10,1... | collective-permute-start | bytes 1572872 | tf_op jit(solution)/shard_map/ppermute | solution.py:223
  99.9 15.2 %collective-permute-start.7 = (f32[64,1792]{1,0:T(8,128)S(1)}, f32[64,1792]{1,0:T(8,128)S(1)}, u32[]{:S(2)}, u32[]{:S(2)}) collective-permute-start(f32[64,1792]{1,0:T(8,128)S(1)} %get-tuple-element.19), channel_id=1, source_target_pairs={{0,2},{1,3},{2,4},{3,5},{4,6},{5,7},{6,8},{7,9},{8,10},{9,11},{10,... | collective-permute-start | bytes 1376264 | tf_op jit(solution)/shard_map/ppermute | solution.py:223

commit v2 on v1

--- a/solution.py
+++ b/solution.py
@@ -138,7 +138,7 @@
     return lax.axis_index("row") * lax.axis_size("col") + lax.axis_index("col")
 
 
-def degree_exchange(devices, parts_ref, out_ref, below, further, above, beyond, send_sem, recv_sem):
+def degree_exchange(devices, parts_ref, degree_ref, own_root, next_root, later_root, below, further, above, beyond, send_sem, recv_sem):
     own = parts_ref.shape[0] // 3
     place = place_of()
     barrier = pltpu.get_barrier_semaphore()
@@ -162,9 +162,18 @@
         copies.append(copy)
     for copy in copies:
         copy.wait()
-    out_ref[0:own] = parts_ref[0:own] + below[0:own] + further[...]
-    out_ref[own : 2 * own] = above[0:own] + parts_ref[own : 2 * own] + below[own : 2 * own]
-    out_ref[2 * own :] = beyond[...] + above[own : 2 * own] + parts_ref[2 * own :]
+    totals = (
+        parts_ref[0:own] + below[0:own] + further[...],
+        above[0:own] + parts_ref[own : 2 * own] + below[own : 2 * own],
+        beyond[...] + above[own : 2 * own] + parts_ref[2 * own :],
+    )
+    extent = parts_ref.shape[1]
+    for total, root_ref in zip(totals, (own_root, next_root, later_root)):
+        root = jnp.sqrt(total)
+        for block in range(root_ref.shape[1] // extent):
+            root_ref[:, block * extent : (block + 1) * extent] = root[block : block + 1]
+    for block in range(own):
+        degree_ref[:, block * extent : (block + 1) * extent] = totals[0][block : block + 1]
 
 
 def sum_kernel(devices, value_ref, out_ref, landed, send_sem, recv_sem):
@@ -228,9 +237,8 @@
     count = tile_count.reshape(1)
     near = neighbors.reshape(slots, nearest, extent)
     weight = weights.reshape(slots, nearest, extent)
-    signs = sketch.astype(jnp.float32)
-    next_signs = moved(signs, -1)
-    later_signs = moved(signs[:, :later_len], -2)
+    next_signs = moved(sketch, -1)
+    later_signs = moved(sketch[:, :later_len], -2)
 
     def tiles(size, *tail):
         return pl.BlockSpec((size,) + tail, lambda i, *_: (i,) + (0,) * len(tail))
@@ -251,20 +259,19 @@
     )(rows, cols, count, near, weight)
     vmem = pl.BlockSpec(memory_space=pltpu.VMEM)
     landing = [pltpu.VMEM((blocks * own_blocks, extent), jnp.float32) for blocks in (2, 1, 2, 1)]
-    degrees = pl.pallas_call(
+    degree, own_root, next_root, later_root = pl.pallas_call(
         functools.partial(degree_exchange, devices),
-        out_shape=jax.ShapeDtypeStruct(parts.shape, jnp.float32),
+        out_shape=[jax.ShapeDtypeStruct((1, length), jnp.float32) for length in (piece, piece, piece, later_len)],
         in_specs=[vmem],
-        out_specs=vmem,
+        out_specs=[vmem] * 4,
         scratch_shapes=landing + [pltpu.SemaphoreType.DMA((4,))] * 2,
         compiler_params=pltpu.CompilerParams(collective_id=1, has_side_effects=True),
         name="degrees",
     )(parts)
-    degree, next_degree, later_degree = degrees.reshape(3, piece)
-    diagonal = degree[None, :] + ridge_term
-    right_side = signs * jnp.sqrt(degree)[None, :]
-    next_side = next_signs * jnp.sqrt(next_degree)[None, :]
-    later_side = later_signs * jnp.sqrt(later_degree)[None, :later_len]
+    diagonal = degree + ridge_term
+    right_side = sketch.astype(jnp.float32) * own_root
+    next_side = next_signs.astype(jnp.float32) * next_root
+    later_side = later_signs.astype(jnp.float32) * later_root
 
     def mirror(vector):
         lengths = (piece, piece, later_len)

time: 134 us -> 141 us (1.052)
  Pallas kernels: 93.8 us -> 103 us
  local copies, waits for them, and re-layouts: 6.91 us -> 4.73 us
    pallas_call x1, Pallas kernels: 14.5 us -> 23.6 us  [shards(): pl.pallas_call(functools.partial(sum_kernel, devices), out_shape=jax.Shap...]
    unnamed x13 -> x12, local copies, waits for them, and re-layouts: 4.19 us -> 2.88 us
  transfers between devices with their start and end apart: 8 -> 8, of which waited for: 1 -> 2; matrix products, arithmetic and copies ran while one was open for 6% -> 4% of each run, Pallas kernels for 59% -> 56%
where the time goes in v2:
time: 141 us
  Pallas kernels  103 us (73%)
  starting transfers between devices  19.6 us (14%)
  other arithmetic  9.55 us (7%)
  local copies, waits for them, and re-layouts  4.73 us (3%)
  waiting for transfers between devices  2.44 us (2%)
  between operations  1.47 us (1%)
    pallas_call x1, Pallas kernels, shards(): pl.pallas_call(build_kernel, grid_spec=pltpu.PrefetchScalarGridSpec(num_s...  30.6 us
    pallas_call x1, Pallas kernels, shards(): pl.pallas_call(functools.partial(sum_kernel, devices), out_shape=jax.Shap...  23.6 us
    ppermute x8, starting transfers between devices, moved(): lax.ppermute(value, axes, [(d, d + steps) for d in range(devices) if 0 <=...  19.6 us
    pallas_call x2, Pallas kernels, mirror(): pl.pallas_call(mirror_kernel, grid_spec=pltpu.PrefetchScalarGridSpec(num_...  19.5 us
    pallas_call x2, Pallas kernels, forward(): pl.pallas_call(forward_kernel, grid_spec=pltpu.PrefetchScalarGridSpec(num...  16.9 us
    pallas_call x1, Pallas kernels, shards(): pl.pallas_call(functools.partial(degree_exchange, devices), out_shape=[ja...  12.2 us
    unnamed x12, local copies, waits for them, and re-layouts  2.88 us
  transfers between devices with their start and end apart: 8, of which 2 were waited for; matrix products, arithmetic and copies ran while one was open for 4% of the time, Pallas kernels for 56%

profile of v2, /device:TPU:0, one launch (start us, length us, event | category | flops | bytes accessed | tf_op | source)
XLA Modules:
  0.0 140.7 jit_solution(2895278358972553159)
XLA Ops:
  0.6 1.3 collective-permute-start
  1.9 1.8 %slice.11 = s32[64,1792]{1,0:T(8,128)} slice(s32[64,2048]{1,0:T(8,128)} %param.6), slice={[0:64], [0:1792]} | slice | bytes 917504 | tf_op jit(solution)/shard_map/slice | solution.py:241
  3.7 1.3 collective-permute-start.1
  5.7 0.7 clamp_bitcast_fusion
  6.4 0.0 copy-start.1
  6.4 1.2 copy-done.1
  7.6 0.0 copy-start.2
  7.6 1.0 copy-done.2
  8.6 0.0 copy-start.3
  8.6 30.6 %build.1 = (bf16[64,256,256]{2,1,0:T(8,128)(2,1)}, bf16[64,256,256]{2,1,0:T(8,128)(2,1)}, f32[24,256]{1,0:T(8,128)S(1)}) custom-call(s32[64]{0:T(128)S(1)} %get-tuple-element.39.rows_ref, s32[64]{0:T(128)S(1)} %get-tuple-element.38.cols_ref, s32[1]{0:T(128)} %bitcast.52.count_ref, s32[64,16,256]{2,1,0:T(8,128)S(1)} %bitcast.53, bf16[64,16,256]{2,1,0:T(8,128)(2,1)S(1)} %bitcast.54), custom_call_target="tpu_custom_call" | custom-call | flops 10000000000 | bytes 25000000 | tf_op jit(solution)/shard_map/build/pallas_call | solution.py:246
  39.3 0.0 copy-start
  39.3 0.6 copy-done
  39.9 12.2 %degrees.1 = (f32[1,2048]{1,0:T(1,128)}, f32[1,2048]{1,0:T(1,128)}, f32[1,2048]{1,0:T(1,128)}, f32[1,1792]{1,0:T(1,128)}) custom-call(f32[24,256]{1,0:T(8,128)} %copy-done), custom_call_target="tpu_custom_call" | custom-call | tf_op jit(solution)/shard_map/degrees/pallas_call | solution.py:262
  52.1 0.0 copy-done.3
  52.1 0.7 convert_multiply_fusion.1.own_ref.vector_ref
  52.9 0.0 copy-start.5
  52.9 9.7 %mirror.2 = (f32[64,2048]{1,0:T(8,128)S(1)}, f32[64,2048]{1,0:T(8,128)S(1)}, f32[64,1792]{1,0:T(8,128)S(1)}) custom-call(s32[64]{0:T(128)S(1)} %get-tuple-element.39.rows_ref, s32[64]{0:T(128)S(1)} %get-tuple-element.38.cols_ref, f32[64,2048]{1,0:T(8,128)S(1)} %convert_multiply_fusion.1.own_ref.vector_ref, bf16[64,256,256]{2,1,0:T(8,128)(2,1)} %get-tuple-element.20.high_ref, ...), custom_call_target="tpu_custom_call" | custom-call | flops 5000000000 | bytes 20000000 | tf_op jit(solution)/shard_map/mirror/pallas_call | solution.py:278
  62.6 4.2 %collective-permute-start.3 = (f32[64,1792]{1,0:T(8,128)S(1)}, f32[64,1792]{1,0:T(8,128)}, u32[]{:S(2)}, u32[]{:S(2)}) collective-permute-start(f32[64,1792]{1,0:T(8,128)S(1)} %get-tuple-element.24), channel_id=1, source_target_pairs={{0,2},{1,3},{2,4},{3,5},{4,6},{5,7},{6,8},{7,9},{8,10},{9,11},{10,... | collective-permute-start | bytes 1376264 | tf_op jit(solution)/shard_map/ppermute | solution.py:232
  66.8 2.1 %collective-permute-start.2 = (f32[64,2048]{1,0:T(8,128)S(1)}, f32[64,2048]{1,0:T(8,128)}, u32[]{:S(2)}, u32[]{:S(2)}) collective-permute-start(f32[64,2048]{1,0:T(8,128)S(1)} %get-tuple-element.23), channel_id=1, source_target_pairs={{0,1},{1,2},{2,3},{3,4},{4,5},{5,6},{6,7},{7,8},{8,9},{9,10},{10,1... | collective-permute-start | bytes 1572872 | tf_op jit(solution)/shard_map/ppermute | solution.py:232
  68.9 0.0 copy-done.5
  68.9 1.3 reduce
  70.2 0.0 collective-permute-done.1
  70.2 0.7 convert_multiply_fusion.2.later_ref
  71.0 0.0 collective-permute-done
  71.0 0.7 convert_multiply_fusion.next_ref
  71.7 0.0 copy-start.4
  71.7 8.5 %forward.2 = f32[64,2048]{1,0:T(8,128)S(1)} custom-call(s32[64]{0:T(128)S(1)} %get-tuple-element.39.rows_ref, s32[64]{0:T(128)S(1)} %get-tuple-element.38.cols_ref, f32[64,2048]{1,0:T(8,128)S(1)} %convert_multiply_fusion.1.own_ref.vector_ref, f32[64,2048]{1,0:T(8,128)S(1)} %convert_multiply_fusion.next_ref, f32[64,1792]{1,0:T(8,128)S(1)} %convert_multiply_fusion.2.later_ref, ...), custom_call_target="tpu_custom_call" | custom-call | flops 5000000000 | bytes 20000000 | tf_op jit(solution)/shard_map/forward/pallas_call | solution.py:297
  80.2 0.0 collective-permute-done.3
  80.2 0.0 collective-permute-done.2
  80.2 0.0 copy-done.4
  80.2 1.3 add_subtract_fusion.1.own_ref.vector_ref
  81.6 1.3 collective-permute-start.4
  82.9 1.3 collective-permute-start.5
  84.2 9.7 %mirror.3 = (f32[64,2048]{1,0:T(8,128)S(1)}, f32[64,2048]{1,0:T(8,128)S(1)}, f32[64,1792]{1,0:T(8,128)S(1)}) custom-call(s32[64]{0:T(128)S(1)} %get-tuple-element.39.rows_ref, s32[64]{0:T(128)S(1)} %get-tuple-element.38.cols_ref, f32[64,2048]{1,0:T(8,128)S(1)} %add_subtract_fusion.1.own_ref.vector_ref, bf16[64,256,256]{2,1,0:T(8,128)(2,1)} %get-tuple-element.20.high_ref, ...), custom_call_target="tpu_custom_call" | custom-call | flops 5000000000 | bytes 20000000 | tf_op jit(solution)/shard_map/mirror/pallas_call | solution.py:278
  94.0 3.1 %collective-permute-start.6 = (f32[64,2048]{1,0:T(8,128)S(1)}, f32[64,2048]{1,0:T(8,128)S(1)}, u32[]{:S(2)}, u32[]{:S(2)}) collective-permute-start(f32[64,2048]{1,0:T(8,128)S(1)} %get-tuple-element.26), channel_id=1, source_target_pairs={{0,1},{1,2},{2,3},{3,4},{4,5},{5,6},{6,7},{7,8},{8,9},{9,10},{10,1... | collective-permute-start | bytes 1572872 | tf_op jit(solution)/shard_map/ppermute | solution.py:232
  97.0 5.1 %collective-permute-start.7 = (f32[64,1792]{1,0:T(8,128)S(1)}, f32[64,1792]{1,0:T(8,128)S(1)}, u32[]{:S(2)}, u32[]{:S(2)}) collective-permute-start(f32[64,1792]{1,0:T(8,128)S(1)} %get-tuple-element.27), channel_id=1, source_target_pairs={{0,2},{1,3},{2,4},{3,5},{4,6},{5,7},{6,8},{7,9},{8,10},{9,11},{10,... | collective-permute-start | bytes 1376264 | tf_op jit(solution)/shard_map/ppermute | solution.py:232
  102.2 0.9 collective-permute-done.5.later_ref
  103.1 0.0 collective-permute-done.4.next_ref
  103.1 8.5 %forward.3 = f32[64,2048]{1,0:T(8,128)S(1)} custom-call(s32[64]{0:T(128)S(1)} %get-tuple-element.39.rows_ref, s32[64]{0:T(128)S(1)} %get-tuple-element.38.cols_ref, f32[64,2048]{1,0:T(8,128)S(1)} %add_subtract_fusion.1.own_ref.vector_ref, f32[64,2048]{1,0:T(8,128)S(1)} %collective-permute-done.4.next_ref, f32[64,1792]{1,0:T(8,128)S(1)} %collective-permute-done.5.later_ref, ...), custom_call_target="tpu_custom_call" | custom-call | flops 5000000000 | bytes 20000000 | tf_op jit(solution)/shard_map/forward/pallas_call | solution.py:297
  111.6 1.5 %collective-permute-done.7 = f32[64,1792]{1,0:T(8,128)S(1)} collective-permute-done((f32[64,1792]{1,0:T(8,128)S(1)}, f32[64,1792]{1,0:T(8,128)S(1)}, u32[]{:S(2)}, u32[]{:S(2)}) %collective-permute-start.7) | collective-permute-done | bytes 458784 | tf_op jit(solution)/shard_map/ppermute | solution.py:232
  113.1 0.0 collective-permute-done.6
  113.1 0.4 multiply_reduce_fusion.3
  113.5 0.6 select_maximum_fusion.value_ref
  114.1 23.6 %total.1 = f32[8,128]{1,0:T(8,128)} custom-call(f32[8,128]{1,0:T(8,128)} %select_maximum_fusion.value_ref), custom_call_target="tpu_custom_call" | custom-call | tf_op jit(solution)/shard_map/total/pallas_call | solution.py:332
  137.7 0.8 fusion.3
  138.5 0.9 fusion.2
  139.3 1.4 multiply_subtract_fusion
  (2 shorter events, 0.0 us)
Async XLA Ops:
  0.6 70.3 %collective-permute-start = (s32[64,2048]{1,0:T(8,128)}, s32[64,2048]{1,0:T(8,128)S(1)}, u32[]{:S(2)}, u32[]{:S(2)}) collective-permute-start(s32[64,2048]{1,0:T(8,128)} %param.6), channel_id=1, source_target_pairs={{1,0},{2,1},{3,2},{4,3},{5,4},{6,5},{7,6},{8,7},{9,8},{10,9},{11,1... | collective-permute-start | bytes 1572872 | tf_op jit(solution)/shard_map/ppermute | solution.py:232
  3.7 66.5 %collective-permute-start.1 = (s32[64,1792]{1,0:T(8,128)}, s32[64,1792]{1,0:T(8,128)S(1)}, u32[]{:S(2)}, u32[]{:S(2)}) collective-permute-start(s32[64,1792]{1,0:T(8,128)} %slice.11), channel_id=1, source_target_pairs={{2,0},{3,1},{4,2},{5,3},{6,4},{7,5},{8,6},{9,7},{10,8},{11,9},{12,... | collective-permute-start | bytes 1376264 | tf_op jit(solution)/shard_map/ppermute | solution.py:232
  6.4 1.2 copy-start.1
  7.6 1.0 copy-start.2
  8.6 43.5 %copy-start.3 = (s32[64,2048]{1,0:T(8,128)S(1)}, s32[64,2048]{1,0:T(8,128)}, u32[]{:S(2)}) copy-start(s32[64,2048]{1,0:T(8,128)} %param.6) | copy-start | bytes 1572868
  39.3 0.6 copy-start
  52.9 16.0 %copy-start.5 = (f32[1,2048]{1,0:T(1,128)S(1)}, f32[1,2048]{1,0:T(1,128)}, u32[]{:S(2)}) copy-start(f32[1,2048]{1,0:T(1,128)} %get-tuple-element.17) | copy-start | bytes 24580
  62.6 17.6 %collective-permute-start.3 = (f32[64,1792]{1,0:T(8,128)S(1)}, f32[64,1792]{1,0:T(8,128)}, u32[]{:S(2)}, u32[]{:S(2)}) collective-permute-start(f32[64,1792]{1,0:T(8,128)S(1)} %get-tuple-element.24), channel_id=1, source_target_pairs={{0,2},{1,3},{2,4},{3,5},{4,6},{5,7},{6,8},{7,9},{8,10},{9,11},{10,... | collective-permute-start | bytes 1376264 | tf_op jit(solution)/shard_map/ppermute | solution.py:232
  66.8 13.4 %collective-permute-start.2 = (f32[64,2048]{1,0:T(8,128)S(1)}, f32[64,2048]{1,0:T(8,128)}, u32[]{:S(2)}, u32[]{:S(2)}) collective-permute-start(f32[64,2048]{1,0:T(8,128)S(1)} %get-tuple-element.23), channel_id=1, source_target_pairs={{0,1},{1,2},{2,3},{3,4},{4,5},{5,6},{6,7},{7,8},{8,9},{9,10},{10,1... | collective-permute-start | bytes 1572872 | tf_op jit(solution)/shard_map/ppermute | solution.py:232
  71.7 8.5 %copy-start.4 = (f32[1,2048]{1,0:T(1,128)S(1)}, f32[1,2048]{1,0:T(1,128)}, u32[]{:S(2)}) copy-start(f32[1,2048]{1,0:T(1,128)} %get-tuple-element.16) | copy-start | bytes 24580
  81.6 21.5 %collective-permute-start.4 = (f32[64,2048]{1,0:T(8,128)S(1)}, f32[64,2048]{1,0:T(8,128)S(1)}, u32[]{:S(2)}, u32[]{:S(2)}) collective-permute-start(f32[64,2048]{1,0:T(8,128)S(1)} %add_subtract_fusion.1.own_ref.vector_ref), channel_id=1, source_target_pairs={{1,0},{2,1},{3,2},{4,3},{5,4},{6,5},{7,6},{8,7},{9,8},{10,9},{11,1... | collective-permute-start | bytes 1572872 | tf_op jit(solution)/shard_map/ppermute | solution.py:232
  82.9 20.2 %collective-permute-start.5 = (f32[64,1792]{1,0:T(8,128)S(1)}, f32[64,1792]{1,0:T(8,128)S(1)}, u32[]{:S(2)}, u32[]{:S(2)}) collective-permute-start(f32[64,1792]{1,0:T(8,128)S(1)} %slice.13), channel_id=1, source_target_pairs={{2,0},{3,1},{4,2},{5,3},{6,4},{7,5},{8,6},{9,7},{10,8},{11,9},{12,... | collective-permute-start | bytes 1376264 | tf_op jit(solution)/shard_map/ppermute | solution.py:232
  94.0 19.1 %collective-permute-start.6 = (f32[64,2048]{1,0:T(8,128)S(1)}, f32[64,2048]{1,0:T(8,128)S(1)}, u32[]{:S(2)}, u32[]{:S(2)}) collective-permute-start(f32[64,2048]{1,0:T(8,128)S(1)} %get-tuple-element.26), channel_id=1, source_target_pairs={{0,1},{1,2},{2,3},{3,4},{4,5},{5,6},{6,7},{7,8},{8,9},{9,10},{10,1... | collective-permute-start | bytes 1572872 | tf_op jit(solution)/shard_map/ppermute | solution.py:232
  97.0 16.1 %collective-permute-start.7 = (f32[64,1792]{1,0:T(8,128)S(1)}, f32[64,1792]{1,0:T(8,128)S(1)}, u32[]{:S(2)}, u32[]{:S(2)}) collective-permute-start(f32[64,1792]{1,0:T(8,128)S(1)} %get-tuple-element.27), channel_id=1, source_target_pairs={{0,2},{1,3},{2,4},{3,5},{4,6},{5,7},{6,8},{7,9},{8,10},{9,11},{10,... | collective-permute-start | bytes 1376264 | tf_op jit(solution)/shard_map/ppermute | solution.py:232

commit v3 on v2

--- a/solution.py
+++ b/solution.py
@@ -237,8 +237,9 @@
     count = tile_count.reshape(1)
     near = neighbors.reshape(slots, nearest, extent)
     weight = weights.reshape(slots, nearest, extent)
-    next_signs = moved(sketch, -1)
-    later_signs = moved(sketch[:, :later_len], -2)
+    signs = sketch.astype(jnp.float32)
+    next_signs = moved(signs, -1)
+    later_signs = moved(signs[:, :later_len], -2)
 
     def tiles(size, *tail):
         return pl.BlockSpec((size,) + tail, lambda i, *_: (i,) + (0,) * len(tail))
@@ -269,9 +270,9 @@
         name="degrees",
     )(parts)
     diagonal = degree + ridge_term
-    right_side = sketch.astype(jnp.float32) * own_root
-    next_side = next_signs.astype(jnp.float32) * next_root
-    later_side = later_signs.astype(jnp.float32) * later_root
+    right_side = signs * own_root
+    next_side = next_signs * next_root
+    later_side = later_signs * later_root
 
     def mirror(vector):
         lengths = (piece, piece, later_len)

time: 141 us -> 142 us (level)
  other arithmetic: 9.55 us -> 11 us
where the time goes in v3:
time: 142 us; the launch traced here: 141 us
  Pallas kernels  103 us (73%)
  starting transfers between devices  19.3 us (14%)
  other arithmetic  11 us (8%)
  local copies, waits for them, and re-layouts  3.71 us (3%)
  waiting for transfers between devices  2.45 us (2%)
  between operations  1.48 us (1%)
    pallas_call x1, Pallas kernels, shards(): pl.pallas_call(build_kernel, grid_spec=pltpu.PrefetchScalarGridSpec(num_s...  30.6 us
    pallas_call x1, Pallas kernels, shards(): pl.pallas_call(functools.partial(sum_kernel, devices), out_shape=jax.Shap...  23.5 us
    pallas_call x2, Pallas kernels, mirror(): pl.pallas_call(mirror_kernel, grid_spec=pltpu.PrefetchScalarGridSpec(num_...  19.5 us
    ppermute x8, starting transfers between devices, moved(): lax.ppermute(value, axes, [(d, d + steps) for d in range(devices) if 0 <=...  19.3 us
    pallas_call x2, Pallas kernels, forward(): pl.pallas_call(forward_kernel, grid_spec=pltpu.PrefetchScalarGridSpec(num...  16.9 us
    pallas_call x1, Pallas kernels, shards(): pl.pallas_call(functools.partial(degree_exchange, devices), out_shape=[ja...  12.2 us
    unnamed x12, local copies, waits for them, and re-layouts  2.88 us
  transfers between devices with their start and end apart: 8, of which 2 were waited for; matrix products, arithmetic and copies ran while one was open for 4% of the time, Pallas kernels for 56%

profile of v3, /device:TPU:0, one launch (start us, length us, event | category | flops | bytes accessed | tf_op | source)
XLA Modules:
  0.0 140.7 jit_solution(15429077328247212902)
XLA Ops:
  0.6 1.1 convert_element_type.8
  1.7 1.3 collective-permute-start
  3.0 0.8 slice.13
  3.8 1.3 collective-permute-start.1
  5.8 0.7 clamp_bitcast_fusion
  6.4 0.0 copy-start.1
  6.4 1.2 copy-done.1
  7.7 0.0 copy-start.2
  7.7 1.0 copy-done.2
  8.7 0.0 copy-start.3
  8.7 30.6 %build.1 = (bf16[64,256,256]{2,1,0:T(8,128)(2,1)}, bf16[64,256,256]{2,1,0:T(8,128)(2,1)}, f32[24,256]{1,0:T(8,128)S(1)}) custom-call(s32[64]{0:T(128)S(1)} %get-tuple-element.39.rows_ref, s32[64]{0:T(128)S(1)} %get-tuple-element.38.cols_ref, s32[1]{0:T(128)} %bitcast.52.count_ref, s32[64,16,256]{2,1,0:T(8,128)S(1)} %bitcast.53, bf16[64,16,256]{2,1,0:T(8,128)(2,1)S(1)} %bitcast.54), custom_call_target="tpu_custom_call" | custom-call | flops 10000000000 | bytes 25000000 | tf_op jit(solution)/shard_map/build/pallas_call | solution.py:247
  39.4 0.0 copy-start
  39.4 0.6 copy-done
  40.0 12.2 %degrees.1 = (f32[1,2048]{1,0:T(1,128)}, f32[1,2048]{1,0:T(1,128)}, f32[1,2048]{1,0:T(1,128)}, f32[1,1792]{1,0:T(1,128)}) custom-call(f32[24,256]{1,0:T(8,128)} %copy-done), custom_call_target="tpu_custom_call" | custom-call | tf_op jit(solution)/shard_map/degrees/pallas_call | solution.py:263
  52.2 0.0 copy-done.3
  52.2 0.7 broadcast_multiply_fusion.1.own_ref.vector_ref
  52.9 0.0 copy-start.5
  52.9 9.7 %mirror.2 = (f32[64,2048]{1,0:T(8,128)S(1)}, f32[64,2048]{1,0:T(8,128)S(1)}, f32[64,1792]{1,0:T(8,128)S(1)}) custom-call(s32[64]{0:T(128)S(1)} %get-tuple-element.39.rows_ref, s32[64]{0:T(128)S(1)} %get-tuple-element.38.cols_ref, f32[64,2048]{1,0:T(8,128)S(1)} %broadcast_multiply_fusion.1.own_ref.vector_ref, ...), custom_call_target="tpu_custom_call" | custom-call | flops 5000000000 | bytes 20000000 | tf_op jit(solution)/shard_map/mirror/pallas_call | solution.py:279
  62.7 4.2 %collective-permute-start.3 = (f32[64,1792]{1,0:T(8,128)S(1)}, f32[64,1792]{1,0:T(8,128)}, u32[]{:S(2)}, u32[]{:S(2)}) collective-permute-start(f32[64,1792]{1,0:T(8,128)S(1)} %get-tuple-element.24), channel_id=1, source_target_pairs={{0,2},{1,3},{2,4},{3,5},{4,6},{5,7},{6,8},{7,9},{8,10},{9,11},{10,... | collective-permute-start | bytes 1376264 | tf_op jit(solution)/shard_map/ppermute | solution.py:232
  66.9 2.1 %collective-permute-start.2 = (f32[64,2048]{1,0:T(8,128)S(1)}, f32[64,2048]{1,0:T(8,128)}, u32[]{:S(2)}, u32[]{:S(2)}) collective-permute-start(f32[64,2048]{1,0:T(8,128)S(1)} %get-tuple-element.23), channel_id=1, source_target_pairs={{0,1},{1,2},{2,3},{3,4},{4,5},{5,6},{6,7},{7,8},{8,9},{9,10},{10,1... | collective-permute-start | bytes 1572872 | tf_op jit(solution)/shard_map/ppermute | solution.py:232
  68.9 0.0 copy-done.5
  69.0 1.3 reduce
  70.3 0.0 collective-permute-done.1
  70.3 0.7 broadcast_multiply_fusion.2.later_ref
  71.0 0.0 collective-permute-done
  71.0 1.1 broadcast_multiply_fusion.next_ref
  72.1 0.0 copy-start.4
  72.1 8.5 %forward.2 = f32[64,2048]{1,0:T(8,128)S(1)} custom-call(s32[64]{0:T(128)S(1)} %get-tuple-element.39.rows_ref, s32[64]{0:T(128)S(1)} %get-tuple-element.38.cols_ref, f32[64,2048]{1,0:T(8,128)S(1)} %broadcast_multiply_fusion.1.own_ref.vector_ref, f32[64,2048]{1,0:T(8,128)S(1)} %broadcast_multiply_fusion.next_ref, ...), custom_call_target="tpu_custom_call" | custom-call | flops 5000000000 | bytes 20000000 | tf_op jit(solution)/shard_map/forward/pallas_call | solution.py:298
  80.6 0.0 collective-permute-done.3
  80.6 0.0 collective-permute-done.2
  80.6 0.0 copy-done.4
  80.6 1.3 add_subtract_fusion.1.own_ref.vector_ref
  82.0 1.3 collective-permute-start.4
  83.3 1.3 collective-permute-start.5
  84.6 9.8 %mirror.3 = (f32[64,2048]{1,0:T(8,128)S(1)}, f32[64,2048]{1,0:T(8,128)S(1)}, f32[64,1792]{1,0:T(8,128)S(1)}) custom-call(s32[64]{0:T(128)S(1)} %get-tuple-element.39.rows_ref, s32[64]{0:T(128)S(1)} %get-tuple-element.38.cols_ref, f32[64,2048]{1,0:T(8,128)S(1)} %add_subtract_fusion.1.own_ref.vector_ref, bf16[64,256,256]{2,1,0:T(8,128)(2,1)} %get-tuple-element.20.high_ref, ...), custom_call_target="tpu_custom_call" | custom-call | flops 5000000000 | bytes 20000000 | tf_op jit(solution)/shard_map/mirror/pallas_call | solution.py:279
  94.4 3.1 %collective-permute-start.6 = (f32[64,2048]{1,0:T(8,128)S(1)}, f32[64,2048]{1,0:T(8,128)S(1)}, u32[]{:S(2)}, u32[]{:S(2)}) collective-permute-start(f32[64,2048]{1,0:T(8,128)S(1)} %get-tuple-element.26), channel_id=1, source_target_pairs={{0,1},{1,2},{2,3},{3,4},{4,5},{5,6},{6,7},{7,8},{8,9},{9,10},{10,1... | collective-permute-start | bytes 1572872 | tf_op jit(solution)/shard_map/ppermute | solution.py:232
  97.4 4.8 %collective-permute-start.7 = (f32[64,1792]{1,0:T(8,128)S(1)}, f32[64,1792]{1,0:T(8,128)S(1)}, u32[]{:S(2)}, u32[]{:S(2)}) collective-permute-start(f32[64,1792]{1,0:T(8,128)S(1)} %get-tuple-element.27), channel_id=1, source_target_pairs={{0,2},{1,3},{2,4},{3,5},{4,6},{5,7},{6,8},{7,9},{8,10},{9,11},{10,... | collective-permute-start | bytes 1376264 | tf_op jit(solution)/shard_map/ppermute | solution.py:232
  102.2 0.9 collective-permute-done.5.later_ref
  103.2 0.0 collective-permute-done.4.next_ref
  103.2 8.5 %forward.3 = f32[64,2048]{1,0:T(8,128)S(1)} custom-call(s32[64]{0:T(128)S(1)} %get-tuple-element.39.rows_ref, s32[64]{0:T(128)S(1)} %get-tuple-element.38.cols_ref, f32[64,2048]{1,0:T(8,128)S(1)} %add_subtract_fusion.1.own_ref.vector_ref, f32[64,2048]{1,0:T(8,128)S(1)} %collective-permute-done.4.next_ref, f32[64,1792]{1,0:T(8,128)S(1)} %collective-permute-done.5.later_ref, ...), custom_call_target="tpu_custom_call" | custom-call | flops 5000000000 | bytes 20000000 | tf_op jit(solution)/shard_map/forward/pallas_call | solution.py:298
  111.7 1.5 %collective-permute-done.7 = f32[64,1792]{1,0:T(8,128)S(1)} collective-permute-done((f32[64,1792]{1,0:T(8,128)S(1)}, f32[64,1792]{1,0:T(8,128)S(1)}, u32[]{:S(2)}, u32[]{:S(2)}) %collective-permute-start.7) | collective-permute-done | bytes 458784 | tf_op jit(solution)/shard_map/ppermute | solution.py:232
  113.2 0.0 collective-permute-done.6
  113.2 0.4 multiply_reduce_fusion.3
  113.5 0.6 select_maximum_fusion.value_ref
  114.1 23.5 %total.1 = f32[8,128]{1,0:T(8,128)} custom-call(f32[8,128]{1,0:T(8,128)} %select_maximum_fusion.value_ref), custom_call_target="tpu_custom_call" | custom-call | tf_op jit(solution)/shard_map/total/pallas_call | solution.py:333
  137.7 0.8 fusion.3
  138.5 0.9 fusion.2
  139.4 1.4 multiply_subtract_fusion
  (2 shorter events, 0.0 us)
Async XLA Ops:
  1.7 69.3 %collective-permute-start = (f32[64,2048]{1,0:T(8,128)S(1)}, f32[64,2048]{1,0:T(8,128)}, u32[]{:S(2)}, u32[]{:S(2)}) collective-permute-start(f32[64,2048]{1,0:T(8,128)S(1)} %convert_element_type.8), channel_id=1, source_target_pairs={{1,0},{2,1},{3,2},{4,3},{5,4},{6,5},{7,6},{8,7},{9,8},{10,9},{11,1... | collective-permute-start | bytes 1572872 | tf_op jit(solution)/shard_map/ppermute | solution.py:232
  3.8 66.5 %collective-permute-start.1 = (f32[64,1792]{1,0:T(8,128)}, f32[64,1792]{1,0:T(8,128)S(1)}, u32[]{:S(2)}, u32[]{:S(2)}) collective-permute-start(f32[64,1792]{1,0:T(8,128)} %slice.13), channel_id=1, source_target_pairs={{2,0},{3,1},{4,2},{5,3},{6,4},{7,5},{8,6},{9,7},{10,8},{11,9},{12,... | collective-permute-start | bytes 1376264 | tf_op jit(solution)/shard_map/ppermute | solution.py:232
  6.4 1.2 copy-start.1
  7.7 1.0 copy-start.2
  8.7 43.5 %copy-start.3 = (s32[64,2048]{1,0:T(8,128)S(1)}, s32[64,2048]{1,0:T(8,128)}, u32[]{:S(2)}) copy-start(s32[64,2048]{1,0:T(8,128)} %param.6) | copy-start | bytes 1572868
  39.4 0.6 copy-start
  52.9 16.0 %copy-start.5 = (f32[1,2048]{1,0:T(1,128)S(1)}, f32[1,2048]{1,0:T(1,128)}, u32[]{:S(2)}) copy-start(f32[1,2048]{1,0:T(1,128)} %get-tuple-element.17) | copy-start | bytes 24580
  62.7 17.9 %collective-permute-start.3 = (f32[64,1792]{1,0:T(8,128)S(1)}, f32[64,1792]{1,0:T(8,128)}, u32[]{:S(2)}, u32[]{:S(2)}) collective-permute-start(f32[64,1792]{1,0:T(8,128)S(1)} %get-tuple-element.24), channel_id=1, source_target_pairs={{0,2},{1,3},{2,4},{3,5},{4,6},{5,7},{6,8},{7,9},{8,10},{9,11},{10,... | collective-permute-start | bytes 1376264 | tf_op jit(solution)/shard_map/ppermute | solution.py:232
  66.9 13.7 %collective-permute-start.2 = (f32[64,2048]{1,0:T(8,128)S(1)}, f32[64,2048]{1,0:T(8,128)}, u32[]{:S(2)}, u32[]{:S(2)}) collective-permute-start(f32[64,2048]{1,0:T(8,128)S(1)} %get-tuple-element.23), channel_id=1, source_target_pairs={{0,1},{1,2},{2,3},{3,4},{4,5},{5,6},{6,7},{7,8},{8,9},{9,10},{10,1... | collective-permute-start | bytes 1572872 | tf_op jit(solution)/shard_map/ppermute | solution.py:232
  72.1 8.5 %copy-start.4 = (f32[1,2048]{1,0:T(1,128)S(1)}, f32[1,2048]{1,0:T(1,128)}, u32[]{:S(2)}) copy-start(f32[1,2048]{1,0:T(1,128)} %get-tuple-element.16) | copy-start | bytes 24580
  82.0 21.2 %collective-permute-start.4 = (f32[64,2048]{1,0:T(8,128)S(1)}, f32[64,2048]{1,0:T(8,128)S(1)}, u32[]{:S(2)}, u32[]{:S(2)}) collective-permute-start(f32[64,2048]{1,0:T(8,128)S(1)} %add_subtract_fusion.1.own_ref.vector_ref), channel_id=1, source_target_pairs={{1,0},{2,1},{3,2},{4,3},{5,4},{6,5},{7,6},{8,7},{9,8},{10,9},{11,1... | collective-permute-start | bytes 1572872 | tf_op jit(solution)/shard_map/ppermute | solution.py:232
  83.3 19.9 %collective-permute-start.5 = (f32[64,1792]{1,0:T(8,128)S(1)}, f32[64,1792]{1,0:T(8,128)S(1)}, u32[]{:S(2)}, u32[]{:S(2)}) collective-permute-start(f32[64,1792]{1,0:T(8,128)S(1)} %slice.14), channel_id=1, source_target_pairs={{2,0},{3,1},{4,2},{5,3},{6,4},{7,5},{8,6},{9,7},{10,8},{11,9},{12,... | collective-permute-start | bytes 1376264 | tf_op jit(solution)/shard_map/ppermute | solution.py:232
  94.4 18.8 %collective-permute-start.6 = (f32[64,2048]{1,0:T(8,128)S(1)}, f32[64,2048]{1,0:T(8,128)S(1)}, u32[]{:S(2)}, u32[]{:S(2)}) collective-permute-start(f32[64,2048]{1,0:T(8,128)S(1)} %get-tuple-element.26), channel_id=1, source_target_pairs={{0,1},{1,2},{2,3},{3,4},{4,5},{5,6},{6,7},{7,8},{8,9},{9,10},{10,1... | collective-permute-start | bytes 1572872 | tf_op jit(solution)/shard_map/ppermute | solution.py:232
  97.4 15.7 %collective-permute-start.7 = (f32[64,1792]{1,0:T(8,128)S(1)}, f32[64,1792]{1,0:T(8,128)S(1)}, u32[]{:S(2)}, u32[]{:S(2)}) collective-permute-start(f32[64,1792]{1,0:T(8,128)S(1)} %get-tuple-element.27), channel_id=1, source_target_pairs={{0,2},{1,3},{2,4},{3,5},{4,6},{5,7},{6,8},{7,9},{8,10},{9,11},{10,... | collective-permute-start | bytes 1376264 | tf_op jit(solution)/shard_map/ppermute | solution.py:232

commit v4 on v1

--- a/solution.py
+++ b/solution.py
@@ -229,8 +229,8 @@
     near = neighbors.reshape(slots, nearest, extent)
     weight = weights.reshape(slots, nearest, extent)
     signs = sketch.astype(jnp.float32)
-    next_signs = moved(signs, -1)
-    later_signs = moved(signs[:, :later_len], -2)
+    next_signs = moved(sketch, -1).astype(jnp.float32)
+    later_signs = moved(sketch[:, :later_len], -2).astype(jnp.float32)
 
     def tiles(size, *tail):
         return pl.BlockSpec((size,) + tail, lambda i, *_: (i,) + (0,) * len(tail))

time: 134 us -> 142 us (1.060)
  Pallas kernels: 93.8 us -> 103 us
  other arithmetic: 10.3 us -> 8.17 us
    pallas_call x1, Pallas kernels: 14.5 us -> 23.3 us  [shards(): pl.pallas_call(functools.partial(sum_kernel, devices), out_shape=jax.Shap...]
  transfers between devices with their start and end apart: 8 -> 8, of which waited for: 1 -> 2; matrix products, arithmetic and copies ran while one was open for 6% -> 6% of each run, Pallas kernels for 59% -> 56%
where the time goes in v4:
time: 142 us; the launch traced here: 141 us
  Pallas kernels  103 us (73%)
  starting transfers between devices  18.7 us (13%)
  other arithmetic  8.17 us (6%)
  local copies, waits for them, and re-layouts  7.93 us (6%)
  waiting for transfers between devices  2.45 us (2%)
  between operations  1.46 us (1%)
    pallas_call x1, Pallas kernels, shards(): pl.pallas_call(build_kernel, grid_spec=pltpu.PrefetchScalarGridSpec(num_s...  30.7 us
    pallas_call x1, Pallas kernels, shards(): pl.pallas_call(functools.partial(sum_kernel, devices), out_shape=jax.Shap...  23.3 us
    pallas_call x2, Pallas kernels, mirror(): pl.pallas_call(mirror_kernel, grid_spec=pltpu.PrefetchScalarGridSpec(num_...  19.5 us
    ppermute x8, starting transfers between devices, moved(): lax.ppermute(value, axes, [(d, d + steps) for d in range(devices) if 0 <=...  18.7 us
    pallas_call x2, Pallas kernels, forward(): pl.pallas_call(forward_kernel, grid_spec=pltpu.PrefetchScalarGridSpec(num...  16.9 us
    pallas_call x1, Pallas kernels, shards(): pl.pallas_call(functools.partial(degree_exchange, devices), out_shape=jax...  12.2 us
    unnamed x13, local copies, waits for them, and re-layouts  4.19 us
  transfers between devices with their start and end apart: 8, of which 2 were waited for; matrix products, arithmetic and copies ran while one was open for 6% of the time, Pallas kernels for 56%

profile of v4, /device:TPU:0, one launch (start us, length us, event | category | flops | bytes accessed | tf_op | source)
XLA Modules:
  0.0 141.3 jit_solution(17618200144850248778)
XLA Ops:
  0.6 1.3 collective-permute-start
  1.9 1.8 %slice.20 = s32[64,1792]{1,0:T(8,128)} slice(s32[64,2048]{1,0:T(8,128)} %param.6), slice={[0:64], [0:1792]} | slice | bytes 917504 | tf_op jit(solution)/shard_map/slice | solution.py:233
  3.7 1.3 collective-permute-start.1
  5.7 0.7 clamp_bitcast_fusion
  6.4 0.0 copy-start.1
  6.4 1.2 copy-done.1
  7.6 0.0 copy-start.2
  7.6 1.0 copy-done.2
  8.6 0.0 copy-start.3
  8.6 30.7 %build.1 = (bf16[64,256,256]{2,1,0:T(8,128)(2,1)}, bf16[64,256,256]{2,1,0:T(8,128)(2,1)}, f32[24,256]{1,0:T(8,128)S(1)}) custom-call(s32[64]{0:T(128)S(1)} %get-tuple-element.35.rows_ref, s32[64]{0:T(128)S(1)} %get-tuple-element.34.cols_ref, s32[1]{0:T(128)} %bitcast.58.count_ref, s32[64,16,256]{2,1,0:T(8,128)S(1)} %bitcast.59, bf16[64,16,256]{2,1,0:T(8,128)(2,1)S(1)} %bitcast.60), custom_call_target="tpu_custom_call" | custom-call | flops 10000000000 | bytes 25000000 | tf_op jit(solution)/shard_map/build/pallas_call | solution.py:238
  39.3 0.0 copy-start
  39.3 0.6 copy-done
  39.9 12.2 %degrees.1 = f32[24,256]{1,0:T(8,128)} custom-call(f32[24,256]{1,0:T(8,128)} %copy-done), custom_call_target="tpu_custom_call" | custom-call | tf_op jit(solution)/shard_map/degrees/pallas_call | solution.py:254
  52.1 1.3 add_bitcast_fusion
  53.5 0.0 copy-done.3
  53.5 9.7 %mirror.2 = (f32[64,2048]{1,0:T(8,128)S(1)}, f32[64,2048]{1,0:T(8,128)S(1)}, f32[64,1792]{1,0:T(8,128)S(1)}) custom-call(s32[64]{0:T(128)S(1)} %get-tuple-element.35.rows_ref, s32[64]{0:T(128)S(1)} %get-tuple-element.34.cols_ref, f32[64,2048]{1,0:T(8,128)S(1)} %convert_multiply_fusion.1.own_ref.vector_ref, bf16[64,256,256]{2,1,0:T(8,128)(2,1)} %get-tuple-element.12.high_ref, ...), custom_call_target="tpu_custom_call" | custom-call | flops 5000000000 | bytes 20000000 | tf_op jit(solution)/shard_map/mirror/pallas_call | solution.py:271
  63.3 4.2 %collective-permute-start.3 = (f32[64,1792]{1,0:T(8,128)S(1)}, f32[64,1792]{1,0:T(8,128)}, u32[]{:S(2)}, u32[]{:S(2)}) collective-permute-start(f32[64,1792]{1,0:T(8,128)S(1)} %get-tuple-element.16), channel_id=1, source_target_pairs={{0,2},{1,3},{2,4},{3,5},{4,6},{5,7},{6,8},{7,9},{8,10},{9,11},{10,... | collective-permute-start | bytes 1376264 | tf_op jit(solution)/shard_map/ppermute | solution.py:223
  67.4 2.1 %collective-permute-start.2 = (f32[64,2048]{1,0:T(8,128)S(1)}, f32[64,2048]{1,0:T(8,128)}, u32[]{:S(2)}, u32[]{:S(2)}) collective-permute-start(f32[64,2048]{1,0:T(8,128)S(1)} %get-tuple-element.15), channel_id=1, source_target_pairs={{0,1},{1,2},{2,3},{3,4},{4,5},{5,6},{6,7},{7,8},{8,9},{9,10},{10,1... | collective-permute-start | bytes 1572872 | tf_op jit(solution)/shard_map/ppermute | solution.py:223
  69.5 0.6 slice_sqrt_fusion
  70.1 0.6 copy.9
  70.7 1.3 slice.22
  72.0 0.7 copy.10
  72.7 0.0 collective-permute-done.1
  72.7 0.7 convert_multiply_fusion.2.later_ref
  73.4 0.0 collective-permute-done
  73.5 0.0 copy-start.4
  73.5 8.5 %forward.2 = f32[64,2048]{1,0:T(8,128)S(1)} custom-call(s32[64]{0:T(128)S(1)} %get-tuple-element.35.rows_ref, s32[64]{0:T(128)S(1)} %get-tuple-element.34.cols_ref, f32[64,2048]{1,0:T(8,128)S(1)} %convert_multiply_fusion.1.own_ref.vector_ref, f32[64,2048]{1,0:T(8,128)S(1)} %convert_multiply_fusion.next_ref, f32[64,1792]{1,0:T(8,128)S(1)} %convert_multiply_fusion.2.later_ref, ...), custom_call_target="tpu_custom_call" | custom-call | flops 5000000000 | bytes 20000000 | tf_op jit(solution)/shard_map/forward/pallas_call | solution.py:290
  82.0 0.0 collective-permute-done.3
  82.0 0.0 collective-permute-done.2
  82.0 0.0 copy-done.4
  82.0 1.3 add_subtract_fusion.1.own_ref.vector_ref
  83.4 1.3 collective-permute-start.4
  84.7 1.3 collective-permute-start.5
  86.0 9.8 %mirror.3 = (f32[64,2048]{1,0:T(8,128)S(1)}, f32[64,2048]{1,0:T(8,128)S(1)}, f32[64,1792]{1,0:T(8,128)S(1)}) custom-call(s32[64]{0:T(128)S(1)} %get-tuple-element.35.rows_ref, s32[64]{0:T(128)S(1)} %get-tuple-element.34.cols_ref, f32[64,2048]{1,0:T(8,128)S(1)} %add_subtract_fusion.1.own_ref.vector_ref, bf16[64,256,256]{2,1,0:T(8,128)(2,1)} %get-tuple-element.12.high_ref, ...), custom_call_target="tpu_custom_call" | custom-call | flops 5000000000 | bytes 20000000 | tf_op jit(solution)/shard_map/mirror/pallas_call | solution.py:271
  95.8 3.1 %collective-permute-start.6 = (f32[64,2048]{1,0:T(8,128)S(1)}, f32[64,2048]{1,0:T(8,128)S(1)}, u32[]{:S(2)}, u32[]{:S(2)}) collective-permute-start(f32[64,2048]{1,0:T(8,128)S(1)} %get-tuple-element.18), channel_id=1, source_target_pairs={{0,1},{1,2},{2,3},{3,4},{4,5},{5,6},{6,7},{7,8},{8,9},{9,10},{10,1... | collective-permute-start | bytes 1572872 | tf_op jit(solution)/shard_map/ppermute | solution.py:223
  98.8 4.3 %collective-permute-start.7 = (f32[64,1792]{1,0:T(8,128)S(1)}, f32[64,1792]{1,0:T(8,128)S(1)}, u32[]{:S(2)}, u32[]{:S(2)}) collective-permute-start(f32[64,1792]{1,0:T(8,128)S(1)} %get-tuple-element.19), channel_id=1, source_target_pairs={{0,2},{1,3},{2,4},{3,5},{4,6},{5,7},{6,8},{7,9},{8,10},{9,11},{10,... | collective-permute-start | bytes 1376264 | tf_op jit(solution)/shard_map/ppermute | solution.py:223
  103.1 0.6 collective-permute-done.5.later_ref
  103.7 0.0 collective-permute-done.4.next_ref
  103.7 8.5 %forward.3 = f32[64,2048]{1,0:T(8,128)S(1)} custom-call(s32[64]{0:T(128)S(1)} %get-tuple-element.35.rows_ref, s32[64]{0:T(128)S(1)} %get-tuple-element.34.cols_ref, f32[64,2048]{1,0:T(8,128)S(1)} %add_subtract_fusion.1.own_ref.vector_ref, f32[64,2048]{1,0:T(8,128)S(1)} %collective-permute-done.4.next_ref, f32[64,1792]{1,0:T(8,128)S(1)} %collective-permute-done.5.later_ref, ...), custom_call_target="tpu_custom_call" | custom-call | flops 5000000000 | bytes 20000000 | tf_op jit(solution)/shard_map/forward/pallas_call | solution.py:290
  112.2 1.8 %collective-permute-done.7 = f32[64,1792]{1,0:T(8,128)S(1)} collective-permute-done((f32[64,1792]{1,0:T(8,128)S(1)}, f32[64,1792]{1,0:T(8,128)S(1)}, u32[]{:S(2)}, u32[]{:S(2)}) %collective-permute-start.7) | collective-permute-done | bytes 458784 | tf_op jit(solution)/shard_map/ppermute | solution.py:223
  114.0 0.0 collective-permute-done.6
  114.0 0.4 multiply_reduce_fusion.3
  114.4 0.6 select_maximum_fusion.value_ref
  115.0 23.3 %total.1 = f32[8,128]{1,0:T(8,128)} custom-call(f32[8,128]{1,0:T(8,128)} %select_maximum_fusion.value_ref), custom_call_target="tpu_custom_call" | custom-call | tf_op jit(solution)/shard_map/total/pallas_call | solution.py:325
  138.3 0.8 fusion.3
  139.1 0.8 fusion.2
  140.0 1.4 multiply_subtract_fusion
  (4 shorter events, 0.1 us)
Async XLA Ops:
  0.6 72.8 %collective-permute-start = (s32[64,2048]{1,0:T(8,128)}, s32[64,2048]{1,0:T(8,128)S(1)}, u32[]{:S(2)}, u32[]{:S(2)}) collective-permute-start(s32[64,2048]{1,0:T(8,128)} %param.6), channel_id=1, source_target_pairs={{1,0},{2,1},{3,2},{4,3},{5,4},{6,5},{7,6},{8,7},{9,8},{10,9},{11,1... | collective-permute-start | bytes 1572872 | tf_op jit(solution)/shard_map/ppermute | solution.py:223
  3.7 69.0 %collective-permute-start.1 = (s32[64,1792]{1,0:T(8,128)}, s32[64,1792]{1,0:T(8,128)S(1)}, u32[]{:S(2)}, u32[]{:S(2)}) collective-permute-start(s32[64,1792]{1,0:T(8,128)} %slice.20), channel_id=1, source_target_pairs={{2,0},{3,1},{4,2},{5,3},{6,4},{7,5},{8,6},{9,7},{10,8},{11,9},{12,... | collective-permute-start | bytes 1376264 | tf_op jit(solution)/shard_map/ppermute | solution.py:223
  6.4 1.2 copy-start.1
  7.6 1.0 copy-start.2
  8.6 44.8 %copy-start.3 = (s32[64,2048]{1,0:T(8,128)S(1)}, s32[64,2048]{1,0:T(8,128)}, u32[]{:S(2)}) copy-start(s32[64,2048]{1,0:T(8,128)} %param.6) | copy-start | bytes 1572868
  39.3 0.6 copy-start
  63.3 18.7 %collective-permute-start.3 = (f32[64,1792]{1,0:T(8,128)S(1)}, f32[64,1792]{1,0:T(8,128)}, u32[]{:S(2)}, u32[]{:S(2)}) collective-permute-start(f32[64,1792]{1,0:T(8,128)S(1)} %get-tuple-element.16), channel_id=1, source_target_pairs={{0,2},{1,3},{2,4},{3,5},{4,6},{5,7},{6,8},{7,9},{8,10},{9,11},{10,... | collective-permute-start | bytes 1376264 | tf_op jit(solution)/shard_map/ppermute | solution.py:223
  67.4 14.6 %collective-permute-start.2 = (f32[64,2048]{1,0:T(8,128)S(1)}, f32[64,2048]{1,0:T(8,128)}, u32[]{:S(2)}, u32[]{:S(2)}) collective-permute-start(f32[64,2048]{1,0:T(8,128)S(1)} %get-tuple-element.15), channel_id=1, source_target_pairs={{0,1},{1,2},{2,3},{3,4},{4,5},{5,6},{6,7},{7,8},{8,9},{9,10},{10,1... | collective-permute-start | bytes 1572872 | tf_op jit(solution)/shard_map/ppermute | solution.py:223
  73.5 8.5 %copy-start.4 = (f32[1,2,8,128]{3,1,2,0:T(2,128)S(1)}, f32[1,2,8,128]{3,1,2,0:T(2,128)}, u32[]{:S(2)}) copy-start(f32[1,2,8,128]{3,1,2,0:T(2,128)} %copy.9) | copy-start | bytes 24580
  83.4 20.3 %collective-permute-start.4 = (f32[64,2048]{1,0:T(8,128)S(1)}, f32[64,2048]{1,0:T(8,128)S(1)}, u32[]{:S(2)}, u32[]{:S(2)}) collective-permute-start(f32[64,2048]{1,0:T(8,128)S(1)} %add_subtract_fusion.1.own_ref.vector_ref), channel_id=1, source_target_pairs={{1,0},{2,1},{3,2},{4,3},{5,4},{6,5},{7,6},{8,7},{9,8},{10,9},{11,1... | collective-permute-start | bytes 1572872 | tf_op jit(solution)/shard_map/ppermute | solution.py:223
  84.7 19.0 %collective-permute-start.5 = (f32[64,1792]{1,0:T(8,128)S(1)}, f32[64,1792]{1,0:T(8,128)S(1)}, u32[]{:S(2)}, u32[]{:S(2)}) collective-permute-start(f32[64,1792]{1,0:T(8,128)S(1)} %slice.25), channel_id=1, source_target_pairs={{2,0},{3,1},{4,2},{5,3},{6,4},{7,5},{8,6},{9,7},{10,8},{11,9},{12,... | collective-permute-start | bytes 1376264 | tf_op jit(solution)/shard_map/ppermute | solution.py:223
  95.8 18.3 %collective-permute-start.6 = (f32[64,2048]{1,0:T(8,128)S(1)}, f32[64,2048]{1,0:T(8,128)S(1)}, u32[]{:S(2)}, u32[]{:S(2)}) collective-permute-start(f32[64,2048]{1,0:T(8,128)S(1)} %get-tuple-element.18), channel_id=1, source_target_pairs={{0,1},{1,2},{2,3},{3,4},{4,5},{5,6},{6,7},{7,8},{8,9},{9,10},{10,1... | collective-permute-start | bytes 1572872 | tf_op jit(solution)/shard_map/ppermute | solution.py:223
  98.8 15.2 %collective-permute-start.7 = (f32[64,1792]{1,0:T(8,128)S(1)}, f32[64,1792]{1,0:T(8,128)S(1)}, u32[]{:S(2)}, u32[]{:S(2)}) collective-permute-start(f32[64,1792]{1,0:T(8,128)S(1)} %get-tuple-element.19), channel_id=1, source_target_pairs={{0,2},{1,3},{2,4},{3,5},{4,6},{5,7},{6,8},{7,9},{8,10},{9,11},{10,... | collective-permute-start | bytes 1376264 | tf_op jit(solution)/shard_map/ppermute | solution.py:223
